TPU v7x, 128 devices: a whole 4x4x4 slice. The times are simulated.
128 devices in a mesh: group: 4 (over y), vocab: 32 (over x, z, core).
Axes of the slice: x: 4, y: 4, z: 4, core: 2. Of those that a mesh axis runs over, the one named last changes fastest.
Arguments:
- hidden: bfloat16 [1024, 7168], P('group', 'vocab'), may hold values from -160 to 160
- main_gain: float32 [7168], replicated, may hold values from 0.1 to 1.9
- head_weight: bfloat16 [7168, 65536], P('group', 'vocab'), may hold values from -1 to 1
- token_owner: int32 [32, 4, 8, 1], P('vocab'), may hold values from 0 to 31; in each aligned block of 32 rows (0 to 31, 32 to 63, ..., all dimensions but the last counted through in order) at most 4 rows name the same one
- token_offset: int32 [32, 4, 8, 1], P('vocab'), may hold values from 0 to 2047
- embed_table: bfloat16 [65536, 7168], P('vocab', 'group'), may hold values from -6 to 6
- hidden_gain: float32 [7168], replicated, may hold values from 0.1 to 1.9
- embed_gain: float32 [7168], replicated, may hold values from 0.1 to 1.9
- hidden_projection: bfloat16 [7168, 7168], P('vocab'), may hold values from -1 to 1
- embed_projection: bfloat16 [7168, 7168], P('vocab'), may hold values from -0.046875 to 0.046875
- draft_gain: float32 [7168], replicated, may hold values from 0.1 to 1.9
Outputs:
- main_logprob: bfloat16 [1024, 65536], P('group', 'vocab')
- draft_logprob: bfloat16 [1024, 65536], P('group', 'vocab')
Inputs may be any that keep to these rules, and one draw needn't show every extreme that they name: `token_owner`: within the rows of one device (aligned blocks of 32 rows taken in order over the first three dimensions) no shard is named more than 4 times, a bound that some block reaches.
All inputs are finite; a program needn't handle non-finite values.
Results may differ from a plain program's by a relative error of at most 0.0035.
Values may be sent and summed in bfloat16 or wider, within the bound.
No kernel may reach another device: no remote copies, remote signals or barrier semaphores. Data moves between devices by JAX's collectives and lax.ppermute only.
A program may use at most 128 MiB of HBM per device.

v0:
```python
import functools

import jax
import jax.numpy as jnp
from jax import lax
from jax.experimental import pallas as pl
from jax.experimental.pallas import tpu as pltpu
from jax.sharding import Mesh, PartitionSpec as P

epsilon = 1e-06
bf16 = jnp.bfloat16
f32 = jnp.float32
VOCAB_AXES = ("x", "z", "core")
SIDE = 4


def shift_pairs(step):
    return [(place, (place + step) % SIDE) for place in range(SIDE)]


def dot(left, right):
    return jnp.dot(left, right, preferred_element_type=f32)


def swap_core(value):
    return lax.ppermute(value, "core", [(0, 1), (1, 0)])


def transpose_plane(value):
    pairs = [(a * SIDE + b, b * SIDE + a) for a in range(SIDE) for b in range(SIDE)]
    return lax.ppermute(value, ("group", "x"), pairs)


def piece_at(value, place, dimension):
    size = value.shape[dimension] // SIDE
    return lax.dynamic_slice_in_dim(value, place * size, size, dimension)


def scatter_sum(value, axis, dimension):
    place = lax.axis_index(axis)
    total = piece_at(value, place, dimension).astype(f32)
    for step in (1, 3, 2):
        sent = piece_at(value, (place + step) % SIDE, dimension).astype(bf16)
        total = total + lax.ppermute(sent, axis, shift_pairs(step)).astype(f32)
    return total


def exchange(value, axis, dimension):
    place = lax.axis_index(axis)
    moved = [piece_at(value, place, dimension)]
    for step in (1, 2, 3):
        sent = piece_at(value, (place + step) % SIDE, dimension)
        moved.append(lax.ppermute(sent, axis, shift_pairs(step)))
    return moved


def in_order(moved, axis, dimension):
    place = lax.axis_index(axis)
    size = moved[0].shape[dimension]
    ordered = [moved[3], moved[2], moved[1], moved[0], moved[3], moved[2], moved[1]]
    stacked = jnp.concatenate(ordered, axis=dimension)
    return lax.dynamic_slice_in_dim(stacked, (3 - place) * size, SIDE * size, dimension)


def gather_along(value, axis, dimension):
    moved = [value] + [lax.ppermute(value, axis, shift_pairs(step)) for step in (1, 2, 3)]
    return in_order(moved, axis, dimension)


def gather_small(value):
    copies = jnp.broadcast_to(value[None], (32,) + value.shape)
    return lax.all_to_all(copies, VOCAB_AXES, split_axis=0, concat_axis=0, tiled=True)


def peak_and_sum(scores):
    peak = jnp.max(scores, axis=1)
    return peak, jnp.sum(jnp.exp(scores - peak[:, None]), axis=1)


def log_sums(peaks, totals):
    top = jnp.max(peaks, axis=0)
    return top + jnp.log(jnp.sum(totals * jnp.exp(peaks - top[None]), axis=0))


def crossed_pairs(step, turn):
    pairs = []
    for x in range(SIDE):
        for z in range(SIDE):
            for core in range(2):
                to_x, to_z = (x + step) % SIDE, (z + step) % SIDE
                target = (to_x, z) if core == turn else (x, to_z)
                pairs.append(((x * SIDE + z) * 2 + core, (target[0] * SIDE + target[1]) * 2 + core))
    return pairs


def crossed(value, step, turn):
    return lax.ppermute(value, VOCAB_AXES, crossed_pairs(step, turn))


def by_core(mine, core):
    theirs = swap_core(mine)
    return jnp.where(core == 0, mine, theirs), jnp.where(core == 0, theirs, mine)


def assemble_kernel(first_hop, places, gain, *refs):
    mine, theirs = refs[:SIDE], refs[SIDE : 2 * SIDE]
    out, squares, held = refs[2 * SIDE :]
    group, core = places[0], places[3]
    block_rows = held.shape[0]
    slab = block_rows // 2

    def one(index, _):
        number, quarter = index // SIDE, lax.rem(index, SIDE)
        hop = number + first_hop
        block = lax.rem(jnp.where(quarter < 2, group - 1 - hop, group + 1 + hop) + 2 * SIDE, SIDE)
        owner = block // 2
        lower = lax.rem(block, 2) == 0
        place = jnp.where(owner == 0, places[1], places[2])
        source = lax.rem(place - quarter + SIDE, SIDE)
        for step in range(SIDE):
            for own, pieces in ((True, mine), (False, theirs)):

                @pl.when((source == step) & ((owner == core) == own))
                def _(ref=pieces[step]):
                    held[...] = ref[...]

        for part in range(slab // 16):
            values = held[part * 32 : (part + 1) * 32, :].astype(f32)
            even = jnp.concatenate([values[0:8], values[16:24]])
            odd = jnp.concatenate([values[8:16], values[24:32]])
            chosen = jnp.where(lower, even, odd)
            rows = pl.ds(pl.multiple_of(quarter * slab + part * 16, 16), 16)
            squares[number, rows, :] = jnp.sum(chosen * chosen, axis=1, keepdims=True)
            out[number, rows, :] = (chosen * gain[...]).astype(bf16)
        return 0

    lax.fori_loop(0, out.shape[0] * SIDE, one, 0)


def assemble(first_hop, count, places, gain, mine, theirs, rows):
    width = gain.shape[0]
    vmem = pl.BlockSpec(memory_space=pltpu.VMEM)
    return pl.pallas_call(
        functools.partial(assemble_kernel, first_hop),
        out_shape=(
            jax.ShapeDtypeStruct((count, rows, width), bf16),
            jax.ShapeDtypeStruct((count, rows, 1), f32),
        ),
        in_specs=[pl.BlockSpec(memory_space=pltpu.SMEM)] + [vmem] * (1 + 2 * SIDE),
        out_specs=(vmem, vmem),
        scratch_shapes=[pltpu.VMEM((rows // 2, width), bf16)],
        compiler_params=pltpu.CompilerParams(vmem_limit_bytes=24 * 1024 * 1024),
        cost_estimate=pl.CostEstimate(
            flops=count * rows * width * 4, bytes_accessed=count * rows * width * 4, transcendentals=0
        ),
    )(places, gain.reshape(1, width), *mine, *theirs)


def embed_kernel(full_width, places, gain, *refs):
    pieces, out = refs[:SIDE], refs[SIDE]
    values = [piece[...].astype(f32) for piece in pieces]
    total = sum(jnp.sum(value * value, axis=1, keepdims=True) for value in values)
    scale = lax.rsqrt(total / full_width + epsilon)
    pair_rows, pair_width = out.shape[1:]
    for step in range(SIDE):
        place = lax.rem(places[0] - step + SIDE, SIDE)
        normed = (values[step] * scale * gain[place]).astype(bf16)
        for z in range(SIDE):
            for core in range(2):
                out[place * 2 * SIDE + z * 2 + core] = normed[
                    core * pair_rows : (core + 1) * pair_rows, z * pair_width : (z + 1) * pair_width
                ]


def embed_slices(places, gain, pieces, full_width, shards):
    look, quarter = pieces[0].shape
    vmem = pl.BlockSpec(memory_space=pltpu.VMEM)
    return pl.pallas_call(
        functools.partial(embed_kernel, full_width),
        out_shape=jax.ShapeDtypeStruct((shards, look // 2, quarter // SIDE), bf16),
        in_specs=[pl.BlockSpec(memory_space=pltpu.SMEM)] + [vmem] * (1 + SIDE),
        out_specs=vmem,
        compiler_params=pltpu.CompilerParams(vmem_limit_bytes=16 * 1024 * 1024),
        cost_estimate=pl.CostEstimate(
            flops=look * full_width * 4, bytes_accessed=look * full_width * 4, transcendentals=0
        ),
    )(places, gain.reshape(SIDE, 1, quarter), *pieces)


def per_device(
    hidden,
    main_gain,
    head_weight,
    token_owner,
    token_offset,
    embed_table,
    hidden_gain,
    embed_gain,
    hidden_projection,
    embed_projection,
    draft_gain,
):
    group = lax.axis_index("group")
    x_place = lax.axis_index("x")
    z_place = lax.axis_index("z")
    core = lax.axis_index("core")
    vocab = (x_place * SIDE + z_place) * 2 + core
    rows, slice_width = hidden.shape
    full_width = main_gain.shape[0]
    quarter = full_width // SIDE

    hidden_values = hidden.astype(f32)

    places = jnp.stack([group, x_place, z_place, core]).astype(jnp.int32)

    main_slice = lax.dynamic_slice_in_dim(main_gain, vocab * slice_width, slice_width, 0)
    main_piece = (hidden_values * main_slice).astype(bf16).T
    main_moved = transpose_plane(main_piece)

    hidden_slice = lax.dynamic_slice_in_dim(hidden_gain, vocab * slice_width, slice_width, 0)
    hidden_piece = (hidden_values * hidden_slice).astype(bf16)
    hidden_moved = [hidden_piece]
    hidden_moved += [lax.ppermute(hidden_piece, "group", shift_pairs(step)) for step in (1, 2, 3)]

    shards = 32
    capacity = 4
    owner_block = token_owner.astype(f32)
    token_block = (owner_block * 2048.0 + token_offset.astype(f32)).reshape(-1)
    look = token_block.shape[0]
    squares = jnp.sum(hidden_values * hidden_values, axis=1)
    gathered = gather_small(jnp.concatenate([token_block, squares]))
    gathered, main_moved, hidden_moved = lax.optimization_barrier(
        (gathered, main_moved, hidden_moved)
    )
    main_stack = lax.all_gather(main_moved, VOCAB_AXES, axis=0, tiled=True).reshape(
        SIDE, quarter, rows
    )
    hidden_scale = lax.rsqrt(jnp.sum(gathered[:, look:], axis=0) / full_width + epsilon)

    block_rows = rows // shards
    pair_rows = 2 * block_rows
    pair_width = 2 * slice_width

    def both_slices(weight):
        mine = lax.dynamic_slice_in_dim(weight, group * quarter, quarter, 1)
        return jnp.concatenate(by_core(mine, core))

    hidden_weight = both_slices(hidden_projection)
    embed_weight = both_slices(embed_projection)

    hidden_all = jnp.stack(hidden_moved)

    def pair_of(stacked, which):
        taken = [
            lax.dynamic_index_in_dim(stacked, (group - 2 * which - e) % SIDE, 0, keepdims=False)
            for e in range(2)
        ]
        return jnp.stack(taken)

    own = pair_of(hidden_all, core)
    other = swap_core(pair_of(hidden_all, 1 - core))
    hidden_pair = jnp.concatenate(
        [jnp.where(core == 0, own, other), jnp.where(core == 0, other, own)], axis=2
    ).reshape(2, shards, block_rows, pair_width)
    hidden_pair = hidden_pair.transpose(1, 0, 2, 3).reshape(shards * pair_rows, pair_width)
    scales = [hidden_scale]
    scales += [lax.ppermute(hidden_scale, "group", shift_pairs(step)) for step in (1, 2, 3)]
    pair_scale = pair_of(jnp.stack(scales), core).reshape(2, shards, block_rows)
    pair_scale = pair_scale.transpose(1, 0, 2).reshape(shards * pair_rows, 1)
    hidden_terms = dot(hidden_pair, hidden_weight) * pair_scale

    tokens = gathered[:, :look].astype(jnp.int32)
    wanted = (tokens // 2048) == vocab
    rank = jnp.cumsum(wanted.astype(jnp.int32), axis=1) - 1
    slot = jnp.arange(capacity, dtype=jnp.int32)
    chosen = wanted[:, None, :] & (rank[:, None, :] == slot[None, :, None])
    requests = jnp.sum(jnp.where(chosen, (tokens % 2048)[:, None, :], 0), axis=2).reshape(-1)
    table_rows = embed_table.shape[0]
    pick = (requests[:, None] == jnp.arange(table_rows, dtype=jnp.int32)[None, :]).astype(bf16)
    found = dot(pick, embed_table).astype(bf16)
    returned = lax.all_to_all(
        found.reshape(shards, capacity, quarter), VOCAB_AXES, split_axis=0, concat_axis=0, tiled=True
    ).reshape(shards * capacity, quarter)
    returned, hidden_terms, embed_weight = lax.optimization_barrier(
        (returned, hidden_terms, embed_weight)
    )
    owners = lax.dynamic_index_in_dim(tokens, vocab, 0, keepdims=False) // 2048
    matches = owners[:, None] == jnp.arange(shards, dtype=jnp.int32)[None, :]
    earlier = jnp.cumsum(matches.astype(jnp.int32), axis=0) - 1
    own_rank = jnp.sum(jnp.where(matches, earlier, 0), axis=1)
    place = owners * capacity + own_rank
    put = (place[:, None] == jnp.arange(shards * capacity, dtype=jnp.int32)[None, :]).astype(bf16)
    fetched = dot(put, returned).astype(bf16)
    fetched_moved = [fetched]
    fetched_moved += [lax.ppermute(fetched, "group", shift_pairs(step)) for step in (1, 2, 3)]
    send = embed_slices(places, embed_gain, fetched_moved, full_width, shards)
    embed_pair = lax.all_to_all(
        send, VOCAB_AXES, split_axis=0, concat_axis=0, tiled=True
    ).reshape(shards * pair_rows, pair_width)

    main_partial = jnp.einsum(
        "gkr,kn->grn", main_stack, head_weight, preferred_element_type=f32
    ).astype(bf16)
    embed_pair, main_partial = lax.optimization_barrier((embed_pair, main_partial))
    main_raw = lax.psum_scatter(
        main_partial.reshape(SIDE * rows, -1), "group", scatter_dimension=0, tiled=True
    )

    state = hidden_terms + dot(embed_pair, embed_weight)
    state_gain = lax.dynamic_slice_in_dim(draft_gain, group * quarter, quarter, 0)
    outer = jnp.where(core == 0, x_place, z_place)
    total = piece_at(state, outer, 0)
    for step in (2, 1, 3):
        sent = piece_at(state, (outer + step) % SIDE, 0).astype(bf16)
        total = total + crossed(sent, step, 0).astype(f32)
    sent = total.astype(bf16)
    for step in (2, 1, 3):
        total = total + crossed(sent, step, 1).astype(f32)
    sent = total.astype(bf16)
    mine = [sent] + [crossed(sent, step, 0) for step in (1, 2, 3)]
    theirs = [swap_core(piece) for piece in mine]
    put_together = functools.partial(
        assemble, places=places, gain=state_gain, mine=mine, theirs=theirs, rows=rows
    )
    half = rows // 2
    first, first_squares = put_together(0, 1)
    carry = [None, None]
    for hop in range(4):
        if hop == 2:
            carry, first_squares, rest_squares = lax.optimization_barrier(
                (carry, first_squares, rest_squares)
            )
            above, below = [], []
            for rows_squares in (first_squares[0], rest_squares[0], rest_squares[1], rest_squares[2]):
                above.append(rows_squares[:half, 0])
                below.append(rows_squares[half:, 0])
            state_squares = jnp.concatenate([above[3], below[3]])
            for step in (1, 2, 3):
                sent = jnp.concatenate([above[3 - step], below[step - 1]])
                state_squares = state_squares + lax.ppermute(sent, "group", shift_pairs(step))
            draft_scale = lax.rsqrt(state_squares / full_width + epsilon)
        terms = dot(first[0] if hop == 0 else rest[hop - 1], head_weight)
        if hop == 0:
            terms, places_later = lax.optimization_barrier((terms.astype(bf16), places))
            rest, rest_squares = put_together(1, 3, places=places_later)
        if hop == 3:
            main_scores = main_raw.astype(f32) * hidden_scale[:, None]
            main_stats = peak_and_sum(main_scores)
            carry, main_stats, draft_scale = lax.optimization_barrier((carry, main_stats, draft_scale))
        terms = [terms[:half], terms[half:]]
        for part in range(2):
            total = terms[part]
            if hop > 0:
                total = total + carry[part].astype(f32)
            if hop < 3:
                total = lax.ppermute(total.astype(bf16), "group", shift_pairs(1 if part == 0 else 3))
            carry[part] = total
    draft_scores = jnp.concatenate(carry) * draft_scale[:, None]
    stats = jnp.concatenate(main_stats + peak_and_sum(draft_scores))
    every = gather_small(stats).reshape(shards, 4, rows)
    main_out = (main_scores - log_sums(every[:, 0], every[:, 1])[:, None]).astype(bf16)
    draft_out = (draft_scores - log_sums(every[:, 2], every[:, 3])[:, None]).astype(bf16)
    return main_out, draft_out


def solution(mesh):
    vocab = mesh.shape["vocab"]
    whole = Mesh(
        mesh.devices.reshape(SIDE, SIDE, vocab // SIDE // 2, 2), ("group", "x", "z", "core")
    )
    placed = (
        P("group", VOCAB_AXES),
        P(),
        P("group", VOCAB_AXES),
        P(VOCAB_AXES, None, None, None),
        P(VOCAB_AXES, None, None, None),
        P(VOCAB_AXES, "group"),
        P(),
        P(),
        P(VOCAB_AXES, None),
        P(VOCAB_AXES, None),
        P(),
    )
    return jax.shard_map(
        per_device,
        mesh=whole,
        in_specs=placed,
        out_specs=(P("group", VOCAB_AXES), P("group", VOCAB_AXES)),
        check_vma=False,
    )
```

profile of v0, /device:TPU:1, one launch (start us, length us, event | category | flops | bytes accessed | tf_op | source)
XLA Modules:
  0.0 239.9 jit_solution(14264482385766168949)
XLA Ops:
  12.1 2.6 %collective-permute-start.2 = (bf16[256,224]{1,0:T(8,128)(2,1)S(1)}, bf16[256,224]{1,0:T(8,128)(2,1)S(1)}, u32[]{:S(2)}, u32[]{:S(2)}) collective-permute-start(bf16[256,224]{1,0:T(8,128)(2,1)S(1)} %get-tuple-element.29), channel_id=1, source_target_pairs={{0,64},{32,96},{64,0},{96,32},{1,65},{33,97},{65,1},{97,33},{2,66}... | collective-permute-start | bytes 344072 | tf_op jit(solution)/shard_map/ppermute | solution.py:223
  17.4 18.1 %all_to_all.25 = f32[32,1,288]{2,1,0:T(1,128)S(1)} all-to-all(f32[32,1,288]{2,1,0:T(1,128)S(1)} %broadcast_in_dim.19), channel_id=1, replica_groups=mesh['group'=4,'x'=4,'z'=4,'core'=2] {'x','z','core'}, dimensions={0} | all-to-all | bytes 73728 | tf_op jit(solution)/shard_map/all_to_all | solution.py:72
  42.0 3.1 %collective-permute-start.7 = (f32[256]{0:T(256)S(1)}, f32[256]{0:T(256)S(1)}, u32[]{:S(2)}, u32[]{:S(2)}) collective-permute-start(f32[256]{0:T(256)S(1)} %add_rsqrt_fusion.1), channel_id=1, source_target_pairs={{0,64},{32,96},{64,0},{96,32},{1,65},{33,97},{65,1},{97,33},{2,66}... | collective-permute-start | bytes 3080 | tf_op jit(solution)/shard_map/ppermute | solution.py:267
  46.7 4.3 %convolution_convert_fusion.1 = bf16[128,1792]{1,0:T(8,128)(2,1)S(1)} fusion(bf16[2048,1792]{1,0:T(8,128)(2,1)} %param.16, s32[128]{0:T(128)S(1)} %eq.92), kind=kOutput, calls=%fused_computation.6 | convolution fusion | flops 940015616 | bytes 7799296 | tf_op jit(solution)/shard_map/dot_general | solution.py:22
  51.9 4.8 %all-to-all-start.1 = ((bf16[32,4,1792]{2,1,0:T(4,128)(2,1)}), bf16[32,4,1792]{2,1,0:T(4,128)(2,1)S(1)}, u32[]{:S(2)}, u32[]{:S(2)}) async-start(bf16[32,4,1792]{2,1,0:T(4,128)(2,1)} %reshape.167), calls=%async_computation.1 | async-start | bytes 917504 | tf_op jit(solution)/shard_map/all_to_all | solution.py:281
  59.3 8.6 %all-to-all-done.1 = bf16[32,4,1792]{2,1,0:T(4,128)(2,1)S(1)} async-done(((bf16[32,4,1792]{2,1,0:T(4,128)(2,1)}), bf16[32,4,1792]{2,1,0:T(4,128)(2,1)S(1)}, u32[]{:S(2)}, u32[]{:S(2)}) %all-to-all-start.1) | async-done | bytes 458784 | tf_op jit(solution)/shard_map/all_to_all | solution.py:281
  71.0 3.0 %convolution_multiply_fusion = f32[512,1792]{1,0:T(8,128)} fusion(bf16[512,448]{1,0:T(8,128)(2,1)S(1)} %bitcast.87, f32[512]{0:T(512)S(1)} %mul.119, bf16[224,1792]{1,0:T(8,128)(2,1)S(1)} %get-tuple-element.78, bf16[224,1792]{1,0:T(8,128)(2,1)S(1)} %get-tuple-element.77), kind=kOutput, calls=%fused_computation.4 | convolution fusion | flops 826212352 | bytes 5736448 | tf_op jit(solution)/shard_map/dot_general | solution.py:22
  77.1 5.8 %collective-permute-done.10.refs_1_ = bf16[32,1792]{1,0:T(8,128)(2,1)S(1)} collective-permute-done((bf16[32,1792]{1,0:T(8,128)(2,1)S(1)}, bf16[32,1792]{1,0:T(8,128)(2,1)S(1)}, u32[]{:S(2)}, u32[]{:S(2)}) %collective-permute-start.10) | collective-permute-done | bytes 114720 | tf_op jit(solution)/shard_map/ppermute | solution.py:295
  85.0 4.4 %all-to-all-start.2 = ((bf16[32,16,448]{2,1,0:T(8,128)(2,1)}), bf16[32,16,448]{2,1,0:T(8,128)(2,1)S(1)}, u32[]{:S(2)}, u32[]{:S(2)}) async-start(bf16[32,16,448]{2,1,0:T(8,128)(2,1)} %shard_map.122), calls=%async_computation.2 | async-start | bytes 1048576 | tf_op jit(solution)/shard_map/all_to_all | solution.py:297
  89.6 12.6 %fusion.2 = bf16[4,256,2048]{2,1,0:T(8,128)(2,1)} fusion(bf16[4,1792,256]{2,1,0:T(8,128)(2,1)} %bitcast.103, bf16[1792,2048]{1,0:T(8,128)(2,1)} %param.13), kind=kOutput, calls=%fused_computation.2 | convolution fusion | flops 7518289920 | bytes 15204352 | tf_op jit(solution)/shard_map/gkr,kn->grn/dot_general | solution.py:301
  102.2 3.2 %convolution_add_fusion = f32[512,1792]{1,0:T(8,128)S(1)} fusion(f32[512,1792]{1,0:T(8,128)} %convolution_multiply_fusion, bf16[512,448]{1,0:T(8,128)(2,1)S(1)} %bitcast.86, bf16[448,1792]{1,0:T(8,128)(2,1)S(1)} %pad_maximum_fusion), kind=kOutput, calls=%fused_computation.3 | convolution fusion | flops 823001088 | bytes 9404416 | tf_op jit(solution)/shard_map/dot_general | solution.py:22
  107.3 3.0 %collective-permute-start.13 = (bf16[128,1792]{1,0:T(8,128)(2,1)S(1)}, bf16[128,1792]{1,0:T(8,128)(2,1)S(1)}, u32[]{:S(2)}, u32[]{:S(2)}) collective-permute-start(bf16[128,1792]{1,0:T(8,128)(2,1)S(1)} %get-tuple-element.66), channel_id=1, source_target_pairs={{0,16},{1,5},{2,18},{3,7},{4,20},{5,1},{6,22},{7,3},{8,24},{9,13},... | collective-permute-start | bytes 1376264 | tf_op jit(solution)/shard_map/ppermute | solution.py:97
  110.6 2.4 collective-permute-start.15
  113.0 3.6 %collective-permute-done.13 = bf16[128,1792]{1,0:T(8,128)(2,1)S(1)} collective-permute-done((bf16[128,1792]{1,0:T(8,128)(2,1)S(1)}, bf16[128,1792]{1,0:T(8,128)(2,1)S(1)}, u32[]{:S(2)}, u32[]{:S(2)}) %collective-permute-start.13) | collective-permute-done | bytes 458784 | tf_op jit(solution)/shard_map/ppermute | solution.py:97
  116.6 5.0 %collective-permute-done.14 = bf16[128,1792]{1,0:T(8,128)(2,1)S(1)} collective-permute-done((bf16[128,1792]{1,0:T(8,128)(2,1)S(1)}, bf16[128,1792]{1,0:T(8,128)(2,1)S(1)}, u32[]{:S(2)}, u32[]{:S(2)}) %collective-permute-start.14) | collective-permute-done | bytes 458784 | tf_op jit(solution)/shard_map/ppermute | solution.py:97
  123.2 2.9 %collective-permute-start.16 = (bf16[128,1792]{1,0:T(8,128)(2,1)S(1)}, bf16[128,1792]{1,0:T(8,128)(2,1)S(1)}, u32[]{:S(2)}, u32[]{:S(2)}) collective-permute-start(bf16[128,1792]{1,0:T(8,128)(2,1)S(1)} %fusion.41), channel_id=1, source_target_pairs={{0,4},{1,17},{2,6},{3,19},{4,0},{5,21},{6,2},{7,23},{8,12},{9,25},... | collective-permute-start | bytes 1376264 | tf_op jit(solution)/shard_map/ppermute | solution.py:97
  128.8 3.7 %collective-permute-done.16 = bf16[128,1792]{1,0:T(8,128)(2,1)S(1)} collective-permute-done((bf16[128,1792]{1,0:T(8,128)(2,1)S(1)}, bf16[128,1792]{1,0:T(8,128)(2,1)S(1)}, u32[]{:S(2)}, u32[]{:S(2)}) %collective-permute-start.16) | collective-permute-done | bytes 458784 | tf_op jit(solution)/shard_map/ppermute | solution.py:97
  132.4 5.0 %collective-permute-done.17 = bf16[128,1792]{1,0:T(8,128)(2,1)S(1)} collective-permute-done((bf16[128,1792]{1,0:T(8,128)(2,1)S(1)}, bf16[128,1792]{1,0:T(8,128)(2,1)S(1)}, u32[]{:S(2)}, u32[]{:S(2)}) %collective-permute-start.17) | collective-permute-done | bytes 458784 | tf_op jit(solution)/shard_map/ppermute | solution.py:97
  143.2 2.7 %collective-permute-start.22 = (bf16[128,1792]{1,0:T(8,128)(2,1)S(1)}, bf16[128,1792]{1,0:T(8,128)(2,1)S(1)}, u32[]{:S(2)}, u32[]{:S(2)}) collective-permute-start(bf16[128,1792]{1,0:T(8,128)(2,1)S(1)} %add_convert_fusion.refs_0_), channel_id=1, source_target_pairs={{0,1},{1,0},{2,3},{3,2},{4,5},{5,4},{6,7},{7,6},{8,9},{9,8},{10,11... | collective-permute-start | bytes 1376264 | tf_op jit(solution)/shard_map/ppermute | solution.py:26
  145.9 2.4 %collective-permute-done.19.refs_1_ = bf16[128,1792]{1,0:T(8,128)(2,1)S(1)} collective-permute-done((bf16[128,1792]{1,0:T(8,128)(2,1)S(1)}, bf16[128,1792]{1,0:T(8,128)(2,1)S(1)}, u32[]{:S(2)}, u32[]{:S(2)}) %collective-permute-start.19) | collective-permute-done | bytes 458784 | tf_op jit(solution)/shard_map/ppermute | solution.py:97
  148.3 2.6 %collective-permute-start.23 = (bf16[128,1792]{1,0:T(8,128)(2,1)S(1)}, bf16[128,1792]{1,0:T(8,128)(2,1)S(1)}, u32[]{:S(2)}, u32[]{:S(2)}) collective-permute-start(bf16[128,1792]{1,0:T(8,128)(2,1)S(1)} %collective-permute-done.19.refs_1_), channel_id=1, source_target_pairs={{0,1},{1,0},{2,3},{3,2},{4,5},{5,4},{6,7},{7,6},{8,9},{9,8},{10,11... | collective-permute-start | bytes 1376264 | tf_op jit(solution)/shard_map/ppermute | solution.py:26
  150.8 3.1 %collective-permute-done.20.refs_2_ = bf16[128,1792]{1,0:T(8,128)(2,1)S(1)} collective-permute-done((bf16[128,1792]{1,0:T(8,128)(2,1)S(1)}, bf16[128,1792]{1,0:T(8,128)(2,1)S(1)}, u32[]{:S(2)}, u32[]{:S(2)}) %collective-permute-start.20) | collective-permute-done | bytes 458784 | tf_op jit(solution)/shard_map/ppermute | solution.py:97
  153.9 2.7 %collective-permute-start.24 = (bf16[128,1792]{1,0:T(8,128)(2,1)S(1)}, bf16[128,1792]{1,0:T(8,128)(2,1)S(1)}, u32[]{:S(2)}, u32[]{:S(2)}) collective-permute-start(bf16[128,1792]{1,0:T(8,128)(2,1)S(1)} %collective-permute-done.20.refs_2_), channel_id=1, source_target_pairs={{0,1},{1,0},{2,3},{3,2},{4,5},{5,4},{6,7},{7,6},{8,9},{9,8},{10,11... | collective-permute-start | bytes 1376264 | tf_op jit(solution)/shard_map/ppermute | solution.py:26
  160.2 5.4 %convolution_convert_fusion = bf16[256,2048]{1,0:T(8,128)(2,1)S(1)} fusion(bf16[1792,2048]{1,0:T(8,128)(2,1)} %param.13, bf16[1,256,1792]{2,1,0:T(8,128)(2,1)S(1)} %get-tuple-element.39), kind=kOutput, calls=%fused_computation.5 | convolution fusion | flops 1879572480 | bytes 9306112 | tf_op jit(solution)/shard_map/dot_general | solution.py:22
  165.8 2.6 %collective-permute-start.28 = (bf16[128,2048]{1,0:T(8,128)(2,1)S(1)}, bf16[128,2048]{1,0:T(8,128)(2,1)S(1)}, u32[]{:S(2)}, u32[]{:S(2)}) collective-permute-start(bf16[128,2048]{1,0:T(8,128)(2,1)S(1)} %get-tuple-element.79), channel_id=1, source_target_pairs={{0,96},{32,0},{64,32},{96,64},{1,97},{33,1},{65,33},{97,65},{2,98}... | collective-permute-start | bytes 1572872 | tf_op jit(solution)/shard_map/ppermute | solution.py:356
  168.4 3.2 %shard_map.124 = (bf16[3,256,1792]{2,1,0:T(8,128)(2,1)S(1)}, f32[3,256,1]{2,1,0:T(8,128)S(1)}) custom-call(s32[4]{0:T(128)S(1)} %pad_add_fusion.places, f32[1,1792]{1,0:T(1,128)S(1)} %reshape.175.gain, bf16[128,1792]{1,0:T(8,128)(2,1)S(1)} %add_convert_fusion.refs_0_, bf16[128,1792]{1,0:T(8,128)(2,1)S(1)} %collective-permute-done.19.refs_1_, ...), custom_call_target="tpu_custom_call" | custom-call | flops 5505024 | bytes 5505024 | tf_op jit(solution)/shard_map/pallas_call | solution.py:143
  175.8 4.3 %collective-permute-done.26 = bf16[128,2048]{1,0:T(8,128)(2,1)S(1)} collective-permute-done((bf16[128,2048]{1,0:T(8,128)(2,1)S(1)}, bf16[128,2048]{1,0:T(8,128)(2,1)S(1)}, u32[]{:S(2)}, u32[]{:S(2)}) %collective-permute-start.26) | collective-permute-done | bytes 524320 | tf_op jit(solution)/shard_map/ppermute | solution.py:356
  183.2 3.4 %fusion.14 = f32[256,2048]{1,0:T(8,128)} fusion(bf16[1792,2048]{1,0:T(8,128)(2,1)S(1)} %bitcast.102, bf16[3,256,1792]{2,1,0:T(8,128)(2,1)S(1)} %get-tuple-element.41), kind=kOutput, calls=%fused_computation.31 | convolution fusion | flops 1879048192 | bytes 10354688 | tf_op jit(solution)/shard_map/dot_general | solution.py:22
  186.6 7.3 %collective-permute-done.27 = bf16[128,2048]{1,0:T(8,128)(2,1)S(1)} collective-permute-done((bf16[128,2048]{1,0:T(8,128)(2,1)S(1)}, bf16[128,2048]{1,0:T(8,128)(2,1)S(1)}, u32[]{:S(2)}, u32[]{:S(2)}) %collective-permute-start.27) | collective-permute-done | bytes 524320 | tf_op jit(solution)/shard_map/ppermute | solution.py:356
  194.4 3.4 %collective-permute-start.33 = (f32[256]{0:T(256)S(1)}, f32[256]{0:T(256)S(1)}, u32[]{:S(2)}, u32[]{:S(2)}) collective-permute-start(f32[256]{0:T(256)S(1)} %pad_maximum_fusion.9), channel_id=1, source_target_pairs={{0,64},{32,96},{64,0},{96,32},{1,65},{33,97},{65,1},{97,33},{2,66}... | collective-permute-start | bytes 3080 | tf_op jit(solution)/shard_map/ppermute | solution.py:340
  204.5 4.9 %collective-permute-done.30 = bf16[128,2048]{1,0:T(8,128)(2,1)S(1)} collective-permute-done((bf16[128,2048]{1,0:T(8,128)(2,1)S(1)}, bf16[128,2048]{1,0:T(8,128)(2,1)S(1)}, u32[]{:S(2)}, u32[]{:S(2)}) %collective-permute-start.30) | collective-permute-done | bytes 524320 | tf_op jit(solution)/shard_map/ppermute | solution.py:356
  212.2 17.7 %all_to_all.26 = f32[32,1,1024]{2,1,0:T(1,128)S(1)} all-to-all(f32[32,1,1024]{2,1,0:T(1,128)S(1)} %broadcast_in_dim.24), channel_id=1, replica_groups=mesh['group'=4,'x'=4,'z'=4,'core'=2] {'x','z','core'}, dimensions={0} | all-to-all | bytes 262144 | tf_op jit(solution)/shard_map/all_to_all | solution.py:72
  (147 shorter events, 63.8 us)
Async XLA Ops:
  7.2 82.4 %all-gather.2.cloned.1.call-start = ((), (), s32[]{:S(2)}) async-start(), calls=%async_computation.5 | async-start | bytes 3784704 | tf_op jit(solution)/shard_map/all_gather | solution.py:235
  9.9 25.6 %collective-permute-start.1 = (bf16[256,224]{1,0:T(8,128)(2,1)S(1)}, bf16[256,224]{1,0:T(8,128)(2,1)S(1)}, u32[]{:S(2)}, u32[]{:S(2)}) collective-permute-start(bf16[256,224]{1,0:T(8,128)(2,1)S(1)} %get-tuple-element.29), channel_id=1, source_target_pairs={{0,32},{32,64},{64,96},{96,0},{1,33},{33,65},{65,97},{97,1},{2,34}... | collective-permute-start | bytes 344072 | tf_op jit(solution)/shard_map/ppermute | solution.py:223
  12.1 23.4 %collective-permute-start.2 = (bf16[256,224]{1,0:T(8,128)(2,1)S(1)}, bf16[256,224]{1,0:T(8,128)(2,1)S(1)}, u32[]{:S(2)}, u32[]{:S(2)}) collective-permute-start(bf16[256,224]{1,0:T(8,128)(2,1)S(1)} %get-tuple-element.29), channel_id=1, source_target_pairs={{0,64},{32,96},{64,0},{96,32},{1,65},{33,97},{65,1},{97,33},{2,66}... | collective-permute-start | bytes 344072 | tf_op jit(solution)/shard_map/ppermute | solution.py:223
  14.7 20.8 %collective-permute-start.3 = (bf16[256,224]{1,0:T(8,128)(2,1)S(1)}, bf16[256,224]{1,0:T(8,128)(2,1)S(1)}, u32[]{:S(2)}, u32[]{:S(2)}) collective-permute-start(bf16[256,224]{1,0:T(8,128)(2,1)S(1)} %get-tuple-element.29), channel_id=1, source_target_pairs={{0,96},{32,0},{64,32},{96,64},{1,97},{33,1},{65,33},{97,65},{2,98}... | collective-permute-start | bytes 344072 | tf_op jit(solution)/shard_map/ppermute | solution.py:223
  15.8 19.7 %collective-permute-start = (bf16[224,256]{0,1:T(8,128)(2,1)S(1)}, bf16[224,256]{0,1:T(8,128)(2,1)S(1)}, u32[]{:S(2)}, u32[]{:S(2)}) collective-permute-start(bf16[224,256]{0,1:T(8,128)(2,1)S(1)} %get-tuple-element.92), channel_id=1, source_target_pairs={{0,0},{8,32},{16,64},{24,96},{32,8},{40,40},{48,72},{56,104},{64,1... | collective-permute-start | bytes 344072 | tf_op jit(solution)/shard_map/ppermute | solution.py:31
  38.4 31.2 %collective-permute-start.5 = (bf16[224,1792]{1,0:T(8,128)(2,1)}, bf16[224,1792]{1,0:T(8,128)(2,1)S(1)}, u32[]{:S(2)}, u32[]{:S(2)}) collective-permute-start(bf16[224,1792]{1,0:T(8,128)(2,1)} %constant_dynamic-slice_fusion.3), channel_id=1, source_target_pairs={{0,1},{1,0},{2,3},{3,2},{4,5},{5,4},{6,7},{7,6},{8,9},{9,8},{10,11... | collective-permute-start | bytes 2408456 | tf_op jit(solution)/shard_map/ppermute | solution.py:26
  40.8 27.2 %collective-permute-start.9 = (bf16[224,1792]{1,0:T(8,128)(2,1)}, bf16[224,1792]{1,0:T(8,128)(2,1)S(1)}, u32[]{:S(2)}, u32[]{:S(2)}) collective-permute-start(bf16[224,1792]{1,0:T(8,128)(2,1)} %constant_dynamic-slice_fusion), channel_id=1, source_target_pairs={{0,1},{1,0},{2,3},{3,2},{4,5},{5,4},{6,7},{7,6},{8,9},{9,8},{10,11... | collective-permute-start | bytes 2408456 | tf_op jit(solution)/shard_map/ppermute | solution.py:26
  41.0 16.3 %collective-permute-start.6 = (f32[256]{0:T(256)S(1)}, f32[256]{0:T(256)S(1)}, u32[]{:S(2)}, u32[]{:S(2)}) collective-permute-start(f32[256]{0:T(256)S(1)} %add_rsqrt_fusion.1), channel_id=1, source_target_pairs={{0,32},{32,64},{64,96},{96,0},{1,33},{33,65},{65,97},{97,1},{2,34}... | collective-permute-start | bytes 3080 | tf_op jit(solution)/shard_map/ppermute | solution.py:267
  42.0 15.8 %collective-permute-start.7 = (f32[256]{0:T(256)S(1)}, f32[256]{0:T(256)S(1)}, u32[]{:S(2)}, u32[]{:S(2)}) collective-permute-start(f32[256]{0:T(256)S(1)} %add_rsqrt_fusion.1), channel_id=1, source_target_pairs={{0,64},{32,96},{64,0},{96,32},{1,65},{33,97},{65,1},{97,33},{2,66}... | collective-permute-start | bytes 3080 | tf_op jit(solution)/shard_map/ppermute | solution.py:267
  45.1 12.7 %collective-permute-start.8 = (f32[256]{0:T(256)S(1)}, f32[256]{0:T(256)S(1)}, u32[]{:S(2)}, u32[]{:S(2)}) collective-permute-start(f32[256]{0:T(256)S(1)} %add_rsqrt_fusion.1), channel_id=1, source_target_pairs={{0,96},{32,0},{64,32},{96,64},{1,97},{33,1},{65,33},{97,65},{2,98}... | collective-permute-start | bytes 3080 | tf_op jit(solution)/shard_map/ppermute | solution.py:267
  51.9 16.0 %all-to-all-start.1 = ((bf16[32,4,1792]{2,1,0:T(4,128)(2,1)}), bf16[32,4,1792]{2,1,0:T(4,128)(2,1)S(1)}, u32[]{:S(2)}, u32[]{:S(2)}) async-start(bf16[32,4,1792]{2,1,0:T(4,128)(2,1)} %reshape.167), calls=%async_computation.1 | async-start | bytes 917504 | tf_op jit(solution)/shard_map/all_to_all | solution.py:281
  74.2 8.7 %collective-permute-start.10 = (bf16[32,1792]{1,0:T(8,128)(2,1)S(1)}, bf16[32,1792]{1,0:T(8,128)(2,1)S(1)}, u32[]{:S(2)}, u32[]{:S(2)}) collective-permute-start(bf16[32,1792]{1,0:T(8,128)(2,1)S(1)} %convolution_convert_fusion.2.refs_0_), channel_id=1, source_target_pairs={{0,32},{32,64},{64,96},{96,0},{1,33},{33,65},{65,97},{97,1},{2,34}... | collective-permute-start | bytes 344072 | tf_op jit(solution)/shard_map/ppermute | solution.py:295
  74.5 8.4 %collective-permute-start.11 = (bf16[32,1792]{1,0:T(8,128)(2,1)S(1)}, bf16[32,1792]{1,0:T(8,128)(2,1)S(1)}, u32[]{:S(2)}, u32[]{:S(2)}) collective-permute-start(bf16[32,1792]{1,0:T(8,128)(2,1)S(1)} %convolution_convert_fusion.2.refs_0_), channel_id=1, source_target_pairs={{0,64},{32,96},{64,0},{96,32},{1,65},{33,97},{65,1},{97,33},{2,66}... | collective-permute-start | bytes 344072 | tf_op jit(solution)/shard_map/ppermute | solution.py:295
  85.0 17.2 %all-to-all-start.2 = ((bf16[32,16,448]{2,1,0:T(8,128)(2,1)}), bf16[32,16,448]{2,1,0:T(8,128)(2,1)S(1)}, u32[]{:S(2)}, u32[]{:S(2)}) async-start(bf16[32,16,448]{2,1,0:T(8,128)(2,1)} %shard_map.122), calls=%async_computation.2 | async-start | bytes 1048576 | tf_op jit(solution)/shard_map/all_to_all | solution.py:297
  89.3 111.8 %reduce-scatter.2.cloned.1.call-start = ((), (), s32[]{:S(2)}) async-start(), calls=%async_computation.6 | async-start | bytes 5242880 | tf_op jit(solution)/shard_map/reduce_scatter | solution.py:305
  107.3 9.3 %collective-permute-start.13 = (bf16[128,1792]{1,0:T(8,128)(2,1)S(1)}, bf16[128,1792]{1,0:T(8,128)(2,1)S(1)}, u32[]{:S(2)}, u32[]{:S(2)}) collective-permute-start(bf16[128,1792]{1,0:T(8,128)(2,1)S(1)} %get-tuple-element.66), channel_id=1, source_target_pairs={{0,16},{1,5},{2,18},{3,7},{4,20},{5,1},{6,22},{7,3},{8,24},{9,13},... | collective-permute-start | bytes 1376264 | tf_op jit(solution)/shard_map/ppermute | solution.py:97
  110.3 11.2 %collective-permute-start.14 = (bf16[128,1792]{1,0:T(8,128)(2,1)S(1)}, bf16[128,1792]{1,0:T(8,128)(2,1)S(1)}, u32[]{:S(2)}, u32[]{:S(2)}) collective-permute-start(bf16[128,1792]{1,0:T(8,128)(2,1)S(1)} %get-tuple-element.68), channel_id=1, source_target_pairs={{0,8},{1,3},{2,10},{3,5},{4,12},{5,7},{6,14},{7,1},{8,16},{9,11},{... | collective-permute-start | bytes 1376264 | tf_op jit(solution)/shard_map/ppermute | solution.py:97
  110.6 11.2 %collective-permute-start.15 = (bf16[128,1792]{1,0:T(8,128)(2,1)S(1)}, bf16[128,1792]{1,0:T(8,128)(2,1)S(1)}, u32[]{:S(2)}, u32[]{:S(2)}) collective-permute-start(bf16[128,1792]{1,0:T(8,128)(2,1)S(1)} %get-tuple-element.67), channel_id=1, source_target_pairs={{0,24},{1,7},{2,26},{3,1},{4,28},{5,3},{6,30},{7,5},{8,0},{9,15},{... | collective-permute-start | bytes 1376264 | tf_op jit(solution)/shard_map/ppermute | solution.py:97
  123.2 9.3 %collective-permute-start.16 = (bf16[128,1792]{1,0:T(8,128)(2,1)S(1)}, bf16[128,1792]{1,0:T(8,128)(2,1)S(1)}, u32[]{:S(2)}, u32[]{:S(2)}) collective-permute-start(bf16[128,1792]{1,0:T(8,128)(2,1)S(1)} %fusion.41), channel_id=1, source_target_pairs={{0,4},{1,17},{2,6},{3,19},{4,0},{5,21},{6,2},{7,23},{8,12},{9,25},... | collective-permute-start | bytes 1376264 | tf_op jit(solution)/shard_map/ppermute | solution.py:97
  126.1 11.4 %collective-permute-start.17 = (bf16[128,1792]{1,0:T(8,128)(2,1)S(1)}, bf16[128,1792]{1,0:T(8,128)(2,1)S(1)}, u32[]{:S(2)}, u32[]{:S(2)}) collective-permute-start(bf16[128,1792]{1,0:T(8,128)(2,1)S(1)} %fusion.41), channel_id=1, source_target_pairs={{0,2},{1,9},{2,4},{3,11},{4,6},{5,13},{6,0},{7,15},{8,10},{9,17},{... | collective-permute-start | bytes 1376264 | tf_op jit(solution)/shard_map/ppermute | solution.py:97
  126.4 11.2 %collective-permute-start.18 = (bf16[128,1792]{1,0:T(8,128)(2,1)S(1)}, bf16[128,1792]{1,0:T(8,128)(2,1)S(1)}, u32[]{:S(2)}, u32[]{:S(2)}) collective-permute-start(bf16[128,1792]{1,0:T(8,128)(2,1)S(1)} %fusion.41), channel_id=1, source_target_pairs={{0,6},{1,25},{2,0},{3,27},{4,2},{5,29},{6,4},{7,31},{8,14},{9,1},{... | collective-permute-start | bytes 1376264 | tf_op jit(solution)/shard_map/ppermute | solution.py:97
  139.3 9.0 %collective-permute-start.19 = (bf16[128,1792]{1,0:T(8,128)(2,1)S(1)}, bf16[128,1792]{1,0:T(8,128)(2,1)S(1)}, u32[]{:S(2)}, u32[]{:S(2)}) collective-permute-start(bf16[128,1792]{1,0:T(8,128)(2,1)S(1)} %add_convert_fusion.refs_0_), channel_id=1, source_target_pairs={{0,8},{1,3},{2,10},{3,5},{4,12},{5,7},{6,14},{7,1},{8,16},{9,11},{... | collective-permute-start | bytes 1376264 | tf_op jit(solution)/shard_map/ppermute | solution.py:97
  140.5 13.4 %collective-permute-start.20 = (bf16[128,1792]{1,0:T(8,128)(2,1)S(1)}, bf16[128,1792]{1,0:T(8,128)(2,1)S(1)}, u32[]{:S(2)}, u32[]{:S(2)}) collective-permute-start(bf16[128,1792]{1,0:T(8,128)(2,1)S(1)} %add_convert_fusion.refs_0_), channel_id=1, source_target_pairs={{0,16},{1,5},{2,18},{3,7},{4,20},{5,1},{6,22},{7,3},{8,24},{9,13},... | collective-permute-start | bytes 1376264 | tf_op jit(solution)/shard_map/ppermute | solution.py:97
  142.9 13.8 %collective-permute-start.21 = (bf16[128,1792]{1,0:T(8,128)(2,1)S(1)}, bf16[128,1792]{1,0:T(8,128)(2,1)S(1)}, u32[]{:S(2)}, u32[]{:S(2)}) collective-permute-start(bf16[128,1792]{1,0:T(8,128)(2,1)S(1)} %add_convert_fusion.refs_0_), channel_id=1, source_target_pairs={{0,24},{1,7},{2,26},{3,1},{4,28},{5,3},{6,30},{7,5},{8,0},{9,15},{... | collective-permute-start | bytes 1376264 | tf_op jit(solution)/shard_map/ppermute | solution.py:97
  143.2 14.3 %collective-permute-start.22 = (bf16[128,1792]{1,0:T(8,128)(2,1)S(1)}, bf16[128,1792]{1,0:T(8,128)(2,1)S(1)}, u32[]{:S(2)}, u32[]{:S(2)}) collective-permute-start(bf16[128,1792]{1,0:T(8,128)(2,1)S(1)} %add_convert_fusion.refs_0_), channel_id=1, source_target_pairs={{0,1},{1,0},{2,3},{3,2},{4,5},{5,4},{6,7},{7,6},{8,9},{9,8},{10,11... | collective-permute-start | bytes 1376264 | tf_op jit(solution)/shard_map/ppermute | solution.py:26
  148.3 9.2 %collective-permute-start.23 = (bf16[128,1792]{1,0:T(8,128)(2,1)S(1)}, bf16[128,1792]{1,0:T(8,128)(2,1)S(1)}, u32[]{:S(2)}, u32[]{:S(2)}) collective-permute-start(bf16[128,1792]{1,0:T(8,128)(2,1)S(1)} %collective-permute-done.19.refs_1_), channel_id=1, source_target_pairs={{0,1},{1,0},{2,3},{3,2},{4,5},{5,4},{6,7},{7,6},{8,9},{9,8},{10,11... | collective-permute-start | bytes 1376264 | tf_op jit(solution)/shard_map/ppermute | solution.py:26
  165.7 14.4 %collective-permute-start.26 = (bf16[128,2048]{1,0:T(8,128)(2,1)S(1)}, bf16[128,2048]{1,0:T(8,128)(2,1)S(1)}, u32[]{:S(2)}, u32[]{:S(2)}) collective-permute-start(bf16[128,2048]{1,0:T(8,128)(2,1)S(1)} %get-tuple-element.80), channel_id=1, source_target_pairs={{0,32},{32,64},{64,96},{96,0},{1,33},{33,65},{65,97},{97,1},{2,34}... | collective-permute-start | bytes 1572872 | tf_op jit(solution)/shard_map/ppermute | solution.py:356
  165.8 14.3 %collective-permute-start.28 = (bf16[128,2048]{1,0:T(8,128)(2,1)S(1)}, bf16[128,2048]{1,0:T(8,128)(2,1)S(1)}, u32[]{:S(2)}, u32[]{:S(2)}) collective-permute-start(bf16[128,2048]{1,0:T(8,128)(2,1)S(1)} %get-tuple-element.79), channel_id=1, source_target_pairs={{0,96},{32,0},{64,32},{96,64},{1,97},{33,1},{65,33},{97,65},{2,98}... | collective-permute-start | bytes 1572872 | tf_op jit(solution)/shard_map/ppermute | solution.py:356
  180.4 13.5 %collective-permute-start.27 = (bf16[128,2048]{1,0:T(8,128)(2,1)S(1)}, bf16[128,2048]{1,0:T(8,128)(2,1)S(1)}, u32[]{:S(2)}, u32[]{:S(2)}) collective-permute-start(bf16[128,2048]{1,0:T(8,128)(2,1)S(1)} %get-tuple-element.74), channel_id=1, source_target_pairs={{0,32},{32,64},{64,96},{96,0},{1,33},{33,65},{65,97},{97,1},{2,34}... | collective-permute-start | bytes 1572872 | tf_op jit(solution)/shard_map/ppermute | solution.py:356
  180.9 13.0 %collective-permute-start.29 = (bf16[128,2048]{1,0:T(8,128)(2,1)S(1)}, bf16[128,2048]{1,0:T(8,128)(2,1)S(1)}, u32[]{:S(2)}, u32[]{:S(2)}) collective-permute-start(bf16[128,2048]{1,0:T(8,128)(2,1)S(1)} %get-tuple-element.73), channel_id=1, source_target_pairs={{0,96},{32,0},{64,32},{96,64},{1,97},{33,1},{65,33},{97,65},{2,98}... | collective-permute-start | bytes 1572872 | tf_op jit(solution)/shard_map/ppermute | solution.py:356
  198.3 11.1 %collective-permute-start.30 = (bf16[128,2048]{1,0:T(8,128)(2,1)S(1)}, bf16[128,2048]{1,0:T(8,128)(2,1)S(1)}, u32[]{:S(2)}, u32[]{:S(2)}) collective-permute-start(bf16[128,2048]{1,0:T(8,128)(2,1)S(1)} %get-tuple-element.72), channel_id=1, source_target_pairs={{0,32},{32,64},{64,96},{96,0},{1,33},{33,65},{65,97},{97,1},{2,34}... | collective-permute-start | bytes 1572872 | tf_op jit(solution)/shard_map/ppermute | solution.py:356
  199.6 9.9 %collective-permute-start.31 = (bf16[128,2048]{1,0:T(8,128)(2,1)S(1)}, bf16[128,2048]{1,0:T(8,128)(2,1)S(1)}, u32[]{:S(2)}, u32[]{:S(2)}) collective-permute-start(bf16[128,2048]{1,0:T(8,128)(2,1)S(1)} %get-tuple-element.71), channel_id=1, source_target_pairs={{0,96},{32,0},{64,32},{96,64},{1,97},{33,1},{65,33},{97,65},{2,98}... | collective-permute-start | bytes 1572872 | tf_op jit(solution)/shard_map/ppermute | solution.py:356
  (12 other events, 89.8 us)
Sparse Core Ops, SparseCore 0:
  36.4 43.8 all-gather.1
  102.3 47.3 reduce-scatter.1
where the time goes:
time: 241 us; the launch traced here: 240 us
  starting transfers between devices  60 us (25%)
  waiting for transfers between devices  56.9 us (24%)
  matrix products  36.2 us (15%)
  blocking collectives  35.8 us (15%)
  other arithmetic  17.9 us (7%)
  between operations  14.5 us (6%)
  local copies, waits for them, and re-layouts  12.2 us (5%)
  Pallas kernels  6.36 us (3%)
    all_to_all x2, blocking collectives, gather_small(): lax.all_to_all(copies, VOCAB_AXES, split_axis=0, concat_axis=0, tiled=True)  35.8 us
    dot_general x8, matrix products, dot(): return jnp.dot(left, right, preferred_element_type=f32)  23.6 us
    ppermute x9, waiting for transfers between devices, crossed(): return lax.ppermute(value, VOCAB_AXES, crossed_pairs(step, turn))  23.2 us
    ppermute x6, waiting for transfers between devices, per_device(): lax.ppermute(total.astype(bf16), 'group', shift_pairs(1 if part == 0 else...  16.6 us
    ppermute x9, starting transfers between devices, crossed(): return lax.ppermute(value, VOCAB_AXES, crossed_pairs(step, turn))  15.1 us
    dot_general x1, matrix products, per_device(): jnp.einsum('gkr,kn->grn', main_stack, head_weight, preferred_element_type...  12.6 us
    ppermute x7, starting transfers between devices, swap_core(): return lax.ppermute(value, 'core', [(0, 1), (1, 0)])  8.89 us
    all_to_all x1, waiting for transfers between devices, per_device(): lax.all_to_all(found.reshape(shards, capacity, quarter), VOCAB_AXES, spli...  8.62 us
  transfers between devices with their start and end apart: 39, of which 18 were waited for; matrix products, arithmetic and copies ran while one was open for 23% of the time, Pallas kernels for 3%

commit v1 on v0

--- a/solution.py
+++ b/solution.py
@@ -112,7 +112,8 @@
     def one(index, _):
         number, quarter = index // SIDE, lax.rem(index, SIDE)
         hop = number + first_hop
-        block = lax.rem(jnp.where(quarter < 2, group - 1 - hop, group + 1 + hop) + 2 * SIDE, SIDE)
+        ahead = jnp.where(hop == 0, 2, jnp.where(hop == 3, 0, jnp.where(hop == 1, 1, -1)))
+        block = lax.rem(group + jnp.where(quarter < 2, -ahead, ahead) + SIDE, SIDE)
         owner = block // 2
         lower = lax.rem(block, 2) == 0
         place = jnp.where(owner == 0, places[1], places[2])
@@ -149,7 +150,7 @@
         in_specs=[pl.BlockSpec(memory_space=pltpu.SMEM)] + [vmem] * (1 + 2 * SIDE),
         out_specs=(vmem, vmem),
         scratch_shapes=[pltpu.VMEM((rows // 2, width), bf16)],
-        compiler_params=pltpu.CompilerParams(vmem_limit_bytes=24 * 1024 * 1024),
+        compiler_params=pltpu.CompilerParams(vmem_limit_bytes=8 * 1024 * 1024),
         cost_estimate=pl.CostEstimate(
             flops=count * rows * width * 4, bytes_accessed=count * rows * width * 4, transcendentals=0
         ),
@@ -180,11 +181,44 @@
         out_shape=jax.ShapeDtypeStruct((shards, look // 2, quarter // SIDE), bf16),
         in_specs=[pl.BlockSpec(memory_space=pltpu.SMEM)] + [vmem] * (1 + SIDE),
         out_specs=vmem,
-        compiler_params=pltpu.CompilerParams(vmem_limit_bytes=16 * 1024 * 1024),
+        compiler_params=pltpu.CompilerParams(vmem_limit_bytes=6 * 1024 * 1024),
         cost_estimate=pl.CostEstimate(
             flops=look * full_width * 4, bytes_accessed=look * full_width * 4, transcendentals=0
         ),
     )(places, gain.reshape(SIDE, 1, quarter), *pieces)
+
+
+def state_kernel(places, hidden_pair, hidden_weight, embed_pair, embed_weight, own, *refs):
+    sent, held = refs[:3], refs[3]
+    rows, width = own.shape
+    outer = jnp.where(places[3] == 0, places[1], places[2])
+    lanes = held.shape[1]
+    for part in range(width // lanes):
+        columns = slice(part * lanes, (part + 1) * lanes)
+        terms = dot(hidden_pair[...], hidden_weight[:, columns])
+        held[...] = terms + dot(embed_pair[...], embed_weight[:, columns])
+        for step, out in ((2, sent[0]), (1, sent[1]), (3, sent[2]), (0, own)):
+            place = lax.rem(outer + step, SIDE)
+            cut = pl.ds(pl.multiple_of(place * rows, rows), rows)
+            out[:, columns] = held[cut, :].astype(out.dtype)
+
+
+def state_blocks(places, hidden_pair, hidden_weight, embed_pair, embed_weight):
+    rows, depth = hidden_pair.shape
+    width = hidden_weight.shape[1]
+    vmem = pl.BlockSpec(memory_space=pltpu.VMEM)
+    block = (rows // SIDE, width)
+    return pl.pallas_call(
+        state_kernel,
+        out_shape=(jax.ShapeDtypeStruct(block, f32),) + (jax.ShapeDtypeStruct(block, bf16),) * 3,
+        in_specs=[pl.BlockSpec(memory_space=pltpu.SMEM)] + [vmem] * 4,
+        out_specs=(vmem,) * 4,
+        scratch_shapes=[pltpu.VMEM((rows, width // 7), f32)],
+        compiler_params=pltpu.CompilerParams(vmem_limit_bytes=10 * 1024 * 1024),
+        cost_estimate=pl.CostEstimate(
+            flops=rows * width * depth * 4, bytes_accessed=depth * width * 8, transcendentals=0
+        ),
+    )(places, hidden_pair, hidden_weight, embed_pair, embed_weight)
 
 
 def per_device(
@@ -215,12 +249,6 @@
 
     main_slice = lax.dynamic_slice_in_dim(main_gain, vocab * slice_width, slice_width, 0)
     main_piece = (hidden_values * main_slice).astype(bf16).T
-    main_moved = transpose_plane(main_piece)
-
-    hidden_slice = lax.dynamic_slice_in_dim(hidden_gain, vocab * slice_width, slice_width, 0)
-    hidden_piece = (hidden_values * hidden_slice).astype(bf16)
-    hidden_moved = [hidden_piece]
-    hidden_moved += [lax.ppermute(hidden_piece, "group", shift_pairs(step)) for step in (1, 2, 3)]
 
     shards = 32
     capacity = 4
@@ -228,46 +256,12 @@
     token_block = (owner_block * 2048.0 + token_offset.astype(f32)).reshape(-1)
     look = token_block.shape[0]
     squares = jnp.sum(hidden_values * hidden_values, axis=1)
-    gathered = gather_small(jnp.concatenate([token_block, squares]))
-    gathered, main_moved, hidden_moved = lax.optimization_barrier(
-        (gathered, main_moved, hidden_moved)
-    )
-    main_stack = lax.all_gather(main_moved, VOCAB_AXES, axis=0, tiled=True).reshape(
-        SIDE, quarter, rows
-    )
+    own_block, main_piece = lax.optimization_barrier(
+        (jnp.concatenate([token_block, squares]), main_piece)
+    )
+    gathered = gather_small(own_block)
+    main_moved = transpose_plane(main_piece)
     hidden_scale = lax.rsqrt(jnp.sum(gathered[:, look:], axis=0) / full_width + epsilon)
-
-    block_rows = rows // shards
-    pair_rows = 2 * block_rows
-    pair_width = 2 * slice_width
-
-    def both_slices(weight):
-        mine = lax.dynamic_slice_in_dim(weight, group * quarter, quarter, 1)
-        return jnp.concatenate(by_core(mine, core))
-
-    hidden_weight = both_slices(hidden_projection)
-    embed_weight = both_slices(embed_projection)
-
-    hidden_all = jnp.stack(hidden_moved)
-
-    def pair_of(stacked, which):
-        taken = [
-            lax.dynamic_index_in_dim(stacked, (group - 2 * which - e) % SIDE, 0, keepdims=False)
-            for e in range(2)
-        ]
-        return jnp.stack(taken)
-
-    own = pair_of(hidden_all, core)
-    other = swap_core(pair_of(hidden_all, 1 - core))
-    hidden_pair = jnp.concatenate(
-        [jnp.where(core == 0, own, other), jnp.where(core == 0, other, own)], axis=2
-    ).reshape(2, shards, block_rows, pair_width)
-    hidden_pair = hidden_pair.transpose(1, 0, 2, 3).reshape(shards * pair_rows, pair_width)
-    scales = [hidden_scale]
-    scales += [lax.ppermute(hidden_scale, "group", shift_pairs(step)) for step in (1, 2, 3)]
-    pair_scale = pair_of(jnp.stack(scales), core).reshape(2, shards, block_rows)
-    pair_scale = pair_scale.transpose(1, 0, 2).reshape(shards * pair_rows, 1)
-    hidden_terms = dot(hidden_pair, hidden_weight) * pair_scale
 
     tokens = gathered[:, :look].astype(jnp.int32)
     wanted = (tokens // 2048) == vocab
@@ -278,12 +272,47 @@
     table_rows = embed_table.shape[0]
     pick = (requests[:, None] == jnp.arange(table_rows, dtype=jnp.int32)[None, :]).astype(bf16)
     found = dot(pick, embed_table).astype(bf16)
+    hidden_slice = lax.dynamic_slice_in_dim(hidden_gain, vocab * slice_width, slice_width, 0)
+    hidden_piece = (hidden_values * hidden_scale[:, None] * hidden_slice).astype(bf16)
+    block_rows = rows // shards
+    pair_rows = 2 * block_rows
+    pair_width = 2 * slice_width
+
+    found, group_later, hidden_piece, main_moved = lax.optimization_barrier(
+        (found, group, hidden_piece, main_moved)
+    )
+    main_stack = lax.all_gather(main_moved, VOCAB_AXES, axis=0, tiled=True).reshape(
+        SIDE, quarter, rows
+    )
+
+    def both_slices(weight):
+        mine = lax.dynamic_slice_in_dim(weight, group_later * quarter, quarter, 1)
+        return jnp.concatenate(by_core(mine, core))
+
+    hidden_weight = both_slices(hidden_projection)
+    embed_weight = both_slices(embed_projection)
+
+    hidden_moved = [hidden_piece]
+    hidden_moved += [lax.ppermute(hidden_piece, "group", shift_pairs(step)) for step in (1, 2, 3)]
+
+    hidden_all = jnp.stack(hidden_moved)
+
+    def pair_of(stacked, which):
+        taken = [
+            lax.dynamic_index_in_dim(stacked, (group - 2 * which - e) % SIDE, 0, keepdims=False)
+            for e in range(2)
+        ]
+        return jnp.stack(taken)
+
+    own = pair_of(hidden_all, core)
+    other = swap_core(pair_of(hidden_all, 1 - core))
+    hidden_pair = jnp.concatenate(
+        [jnp.where(core == 0, own, other), jnp.where(core == 0, other, own)], axis=2
+    ).reshape(2, shards, block_rows, pair_width)
+    hidden_pair = hidden_pair.transpose(1, 0, 2, 3).reshape(shards * pair_rows, pair_width)
     returned = lax.all_to_all(
         found.reshape(shards, capacity, quarter), VOCAB_AXES, split_axis=0, concat_axis=0, tiled=True
     ).reshape(shards * capacity, quarter)
-    returned, hidden_terms, embed_weight = lax.optimization_barrier(
-        (returned, hidden_terms, embed_weight)
-    )
     owners = lax.dynamic_index_in_dim(tokens, vocab, 0, keepdims=False) // 2048
     matches = owners[:, None] == jnp.arange(shards, dtype=jnp.int32)[None, :]
     earlier = jnp.cumsum(matches.astype(jnp.int32), axis=0) - 1
@@ -293,26 +322,29 @@
     fetched = dot(put, returned).astype(bf16)
     fetched_moved = [fetched]
     fetched_moved += [lax.ppermute(fetched, "group", shift_pairs(step)) for step in (1, 2, 3)]
+    fetched_moved, hidden_weight, embed_weight, hidden_pair = lax.optimization_barrier(
+        (fetched_moved, hidden_weight, embed_weight, hidden_pair)
+    )
     send = embed_slices(places, embed_gain, fetched_moved, full_width, shards)
     embed_pair = lax.all_to_all(
         send, VOCAB_AXES, split_axis=0, concat_axis=0, tiled=True
     ).reshape(shards * pair_rows, pair_width)
 
+    state_gain = lax.dynamic_slice_in_dim(draft_gain, group * quarter, quarter, 0)
+
+    total, *sent = state_blocks(
+        places, hidden_pair, hidden_weight, embed_pair, embed_weight
+    )
+    moved = [crossed(block, step, 0) for block, step in zip(sent, (2, 1, 3))]
     main_partial = jnp.einsum(
         "gkr,kn->grn", main_stack, head_weight, preferred_element_type=f32
     ).astype(bf16)
-    embed_pair, main_partial = lax.optimization_barrier((embed_pair, main_partial))
+    moved, main_partial = lax.optimization_barrier((moved, main_partial))
     main_raw = lax.psum_scatter(
         main_partial.reshape(SIDE * rows, -1), "group", scatter_dimension=0, tiled=True
     )
-
-    state = hidden_terms + dot(embed_pair, embed_weight)
-    state_gain = lax.dynamic_slice_in_dim(draft_gain, group * quarter, quarter, 0)
-    outer = jnp.where(core == 0, x_place, z_place)
-    total = piece_at(state, outer, 0)
-    for step in (2, 1, 3):
-        sent = piece_at(state, (outer + step) % SIDE, 0).astype(bf16)
-        total = total + crossed(sent, step, 0).astype(f32)
+    for piece in moved:
+        total = total + piece.astype(f32)
     sent = total.astype(bf16)
     for step in (2, 1, 3):
         total = total + crossed(sent, step, 1).astype(f32)
@@ -323,39 +355,53 @@
         assemble, places=places, gain=state_gain, mine=mine, theirs=theirs, rows=rows
     )
     half = rows // 2
-    first, first_squares = put_together(0, 1)
-    carry = [None, None]
-    for hop in range(4):
-        if hop == 2:
-            carry, first_squares, rest_squares = lax.optimization_barrier(
-                (carry, first_squares, rest_squares)
+    (far, near), (far_squares, near_squares) = put_together(0, 2)
+    far_terms = dot(far, head_weight).astype(bf16)
+    far_up = lax.ppermute(far_terms[:half], "group", shift_pairs(1))
+    far_down = lax.ppermute(far_terms[half:], "group", shift_pairs(3))
+    near_terms = dot(near, head_weight).astype(bf16)
+    near_up = lax.ppermute(near_terms[half:], "group", shift_pairs(1))
+    near_down = lax.ppermute(near_terms[:half], "group", shift_pairs(3))
+    near_terms, places_later = lax.optimization_barrier((near_terms, places))
+    (passing, own), (passing_squares, own_squares) = put_together(2, 2, places=places_later)
+    passing_terms = dot(passing, head_weight)
+    passing_up = (passing_terms[:half] + far_up.astype(f32)).astype(bf16)
+    passing_down = (passing_terms[half:] + far_down.astype(f32)).astype(bf16)
+    passed_up = lax.ppermute(passing_up, "group", shift_pairs(1))
+    passed_down = lax.ppermute(passing_down, "group", shift_pairs(3))
+    own_terms = dot(own, head_weight)
+    near_up, near_down, main_raw, far_squares, near_squares, passing_squares, _, _ = (
+        lax.optimization_barrier(
+            (
+                near_up,
+                near_down,
+                main_raw,
+                far_squares,
+                near_squares,
+                passing_squares,
+                passing_up,
+                passing_down,
             )
-            above, below = [], []
-            for rows_squares in (first_squares[0], rest_squares[0], rest_squares[1], rest_squares[2]):
-                above.append(rows_squares[:half, 0])
-                below.append(rows_squares[half:, 0])
-            state_squares = jnp.concatenate([above[3], below[3]])
-            for step in (1, 2, 3):
-                sent = jnp.concatenate([above[3 - step], below[step - 1]])
-                state_squares = state_squares + lax.ppermute(sent, "group", shift_pairs(step))
-            draft_scale = lax.rsqrt(state_squares / full_width + epsilon)
-        terms = dot(first[0] if hop == 0 else rest[hop - 1], head_weight)
-        if hop == 0:
-            terms, places_later = lax.optimization_barrier((terms.astype(bf16), places))
-            rest, rest_squares = put_together(1, 3, places=places_later)
-        if hop == 3:
-            main_scores = main_raw.astype(f32) * hidden_scale[:, None]
-            main_stats = peak_and_sum(main_scores)
-            carry, main_stats, draft_scale = lax.optimization_barrier((carry, main_stats, draft_scale))
-        terms = [terms[:half], terms[half:]]
-        for part in range(2):
-            total = terms[part]
-            if hop > 0:
-                total = total + carry[part].astype(f32)
-            if hop < 3:
-                total = lax.ppermute(total.astype(bf16), "group", shift_pairs(1 if part == 0 else 3))
-            carry[part] = total
-    draft_scores = jnp.concatenate(carry) * draft_scale[:, None]
+        )
+    )
+    near_squares, passing_squares = near_squares[:, 0], passing_squares[:, 0]
+    state_squares = own_squares[:, 0]
+    for step, sent in (
+        (1, jnp.concatenate([passing_squares[:half], near_squares[half:]])),
+        (3, jnp.concatenate([near_squares[:half], passing_squares[half:]])),
+        (2, far_squares[:, 0]),
+    ):
+        state_squares = state_squares + lax.ppermute(sent, "group", shift_pairs(step))
+    draft_scale = lax.rsqrt(state_squares / full_width + epsilon)
+    main_scores = main_raw.astype(f32) * hidden_scale[:, None]
+    main_stats = peak_and_sum(main_scores)
+    upper = own_terms[:half] + near_down.astype(f32)
+    lower = own_terms[half:] + near_up.astype(f32)
+    upper, lower, main_stats, draft_scale, passed_up, passed_down = lax.optimization_barrier(
+        (upper, lower, main_stats, draft_scale, passed_up, passed_down)
+    )
+    draft_scores = jnp.concatenate([upper + passed_up.astype(f32), lower + passed_down.astype(f32)])
+    draft_scores = draft_scores * draft_scale[:, None]
     stats = jnp.concatenate(main_stats + peak_and_sum(draft_scores))
     every = gather_small(stats).reshape(shards, 4, rows)
     main_out = (main_scores - log_sums(every[:, 0], every[:, 1])[:, None]).astype(bf16)

time: 241 us -> 218 us (0.905)
  blocking collectives: 35.8 us -> 27.6 us
  matrix products: 36.2 us -> 28.6 us
  starting transfers between devices: 60 us -> 53.3 us
  Pallas kernels: 6.36 us -> 9.69 us
    all_to_all x2 -> x1, blocking collectives: 35.8 us -> 12.1 us  [gather_small(): lax.all_to_all(copies, VOCAB_AXES, split_axis=0, concat_axis=0, tiled=True)]
    all_to_all x0 -> x1, blocking collectives: none -> 15.5 us  [per_device(): lax.all_to_all(send, VOCAB_AXES, split_axis=0, concat_axis=0, tiled=True)]
    dot_general x8 -> x6, matrix products: 23.6 us -> 16.1 us  [dot(): return jnp.dot(left, right, preferred_element_type=f32)]
    ppermute x9, starting transfers between devices: 15.1 us -> 7.87 us  [crossed(): return lax.ppermute(value, VOCAB_AXES, crossed_pairs(step, turn))]
    ppermute x9 -> x6, starting transfers between devices: 13.3 us -> 6.08 us  [the longest x1 2.96 us: per_device(): near_down = lax.ppermute(near_terms[:half], 'group', shift_pairs(3))]
    ppermute x3, waiting for transfers between devices: 0.01 us -> 7.09 us  [per_device(): lax.ppermute(sent, 'group', shift_pairs(step))]
    all_to_all x1, waiting for transfers between devices: 0.01 us -> 5.81 us  [gather_small(): lax.all_to_all(copies, VOCAB_AXES, split_axis=0, concat_axis=0, tiled=True)]
    ppermute x9, waiting for transfers between devices: 23.2 us -> 17.6 us  [crossed(): return lax.ppermute(value, VOCAB_AXES, crossed_pairs(step, turn))]
  transfers between devices with their start and end apart: 39 -> 36, of which waited for: 18 -> 15; matrix products, arithmetic and copies ran while one was open for 23% -> 21% of each run, Pallas kernels for 3% -> 4%
where the time goes in v1:
time: 218 us; the launch traced here: 217 us
  waiting for transfers between devices  54.7 us (25%)
  starting transfers between devices  53.3 us (24%)
  matrix products  28.6 us (13%)
  blocking collectives  27.6 us (13%)
  other arithmetic  18.3 us (8%)
  between operations  14.6 us (7%)
  local copies, waits for them, and re-layouts  10.1 us (5%)
  Pallas kernels  9.69 us (4%)
    ppermute x9, waiting for transfers between devices, crossed(): return lax.ppermute(value, VOCAB_AXES, crossed_pairs(step, turn))  17.6 us
    dot_general x6, matrix products, dot(): return jnp.dot(left, right, preferred_element_type=f32)  16.1 us
    all_to_all x1, blocking collectives, per_device(): lax.all_to_all(send, VOCAB_AXES, split_axis=0, concat_axis=0, tiled=True)  15.5 us
    dot_general x1, matrix products, per_device(): jnp.einsum('gkr,kn->grn', main_stack, head_weight, preferred_element_type...  12.5 us
    ppermute x7, starting transfers between devices, swap_core(): return lax.ppermute(value, 'core', [(0, 1), (1, 0)])  12.1 us
    all_to_all x1, blocking collectives, gather_small(): lax.all_to_all(copies, VOCAB_AXES, split_axis=0, concat_axis=0, tiled=True)  12.1 us
    all_to_all x1, starting transfers between devices, gather_small(): lax.all_to_all(copies, VOCAB_AXES, split_axis=0, concat_axis=0, tiled=True)  9.43 us
    ppermute x9, starting transfers between devices, crossed(): return lax.ppermute(value, VOCAB_AXES, crossed_pairs(step, turn))  7.87 us
  transfers between devices with their start and end apart: 36, of which 15 were waited for; matrix products, arithmetic and copies ran while one was open for 21% of the time, Pallas kernels for 4%

profile of v1, /device:TPU:1, one launch (start us, length us, event | category | flops | bytes accessed | tf_op | source)
XLA Modules:
  0.0 216.8 jit_solution(1619630408820849457)
XLA Ops:
  10.6 9.4 %all-to-all-start = ((f32[32,1,288]{2,1,0:T(1,128)}), f32[32,1,288]{2,1,0:T(1,128)S(1)}, u32[]{:S(2)}, u32[]{:S(2)}) async-start(f32[32,1,288]{2,1,0:T(1,128)} %broadcast_in_dim.19), calls=%async_computation | async-start | bytes 98304 | tf_op jit(solution)/shard_map/all_to_all | solution.py:72
  21.6 5.8 %all-to-all-done = f32[32,1,288]{2,1,0:T(1,128)S(1)} async-done(((f32[32,1,288]{2,1,0:T(1,128)}), f32[32,1,288]{2,1,0:T(1,128)S(1)}, u32[]{:S(2)}, u32[]{:S(2)}) %all-to-all-start) | async-done | bytes 36896 | tf_op jit(solution)/shard_map/all_to_all | solution.py:72
  28.1 4.3 %convolution_convert_fusion.2 = bf16[128,1792]{1,0:T(8,128)(2,1)S(1)} fusion(bf16[2048,1792]{1,0:T(8,128)(2,1)} %param.16, s32[128]{0:T(128)S(1)} %eq.86), kind=kOutput, calls=%fused_computation.5 | convolution fusion | flops 940015616 | bytes 7799296 | tf_op jit(solution)/shard_map/dot_general | solution.py:22
  33.8 3.5 %collective-permute-start.8 = (bf16[256,224]{1,0:T(8,128)(2,1)S(1)}, bf16[256,224]{1,0:T(8,128)(2,1)S(1)}, u32[]{:S(2)}, u32[]{:S(2)}) collective-permute-start(bf16[256,224]{1,0:T(8,128)(2,1)S(1)} %fusion.23), channel_id=1, source_target_pairs={{0,96},{32,0},{64,32},{96,64},{1,97},{33,1},{65,33},{97,65},{2,98}... | collective-permute-start | bytes 344072 | tf_op jit(solution)/shard_map/ppermute | solution.py:296
  38.8 6.6 %all-to-all-start.1 = ((bf16[32,4,1792]{2,1,0:T(4,128)(2,1)}), bf16[32,4,1792]{2,1,0:T(4,128)(2,1)S(1)}, u32[]{:S(2)}, u32[]{:S(2)}) async-start(bf16[32,4,1792]{2,1,0:T(4,128)(2,1)} %reshape.132), calls=%async_computation.1 | async-start | bytes 917504 | tf_op jit(solution)/shard_map/all_to_all | solution.py:313
  47.6 2.1 constant_dynamic-slice_fusion.4
  50.2 7.1 %all-to-all-done.1 = bf16[32,4,1792]{2,1,0:T(4,128)(2,1)S(1)} async-done(((bf16[32,4,1792]{2,1,0:T(4,128)(2,1)}), bf16[32,4,1792]{2,1,0:T(4,128)(2,1)S(1)}, u32[]{:S(2)}, u32[]{:S(2)}) %all-to-all-start.1) | async-done | bytes 458784 | tf_op jit(solution)/shard_map/all_to_all | solution.py:313
  57.6 2.9 %collective-permute-start.3 = (bf16[32,1792]{1,0:T(8,128)(2,1)S(1)}, bf16[32,1792]{1,0:T(8,128)(2,1)S(1)}, u32[]{:S(2)}, u32[]{:S(2)}) collective-permute-start(bf16[32,1792]{1,0:T(8,128)(2,1)S(1)} %convolution_convert_fusion.3.refs_0_), channel_id=1, source_target_pairs={{0,96},{32,0},{64,32},{96,64},{1,97},{33,1},{65,33},{97,65},{2,98}... | collective-permute-start | bytes 344072 | tf_op jit(solution)/shard_map/ppermute | solution.py:324
  66.8 2.9 %collective-permute-done.1.refs_1_ = bf16[32,1792]{1,0:T(8,128)(2,1)S(1)} collective-permute-done((bf16[32,1792]{1,0:T(8,128)(2,1)S(1)}, bf16[32,1792]{1,0:T(8,128)(2,1)S(1)}, u32[]{:S(2)}, u32[]{:S(2)}) %collective-permute-start.1) | collective-permute-done | bytes 114720 | tf_op jit(solution)/shard_map/ppermute | solution.py:324
  70.6 15.5 %all_to_all.25 = bf16[32,16,448]{2,1,0:T(8,128)(2,1)S(1)} all-to-all(bf16[32,16,448]{2,1,0:T(8,128)(2,1)S(1)} %shard_map.122), channel_id=1, replica_groups=mesh['group'=4,'x'=4,'z'=4,'core'=2] {'x','z','core'}, dimensions={0} | all-to-all | bytes 917504 | tf_op jit(solution)/shard_map/all_to_all | solution.py:329
  86.1 3.0 %shard_map.123 = (f32[128,1792]{1,0:T(8,128)S(1)}, bf16[128,1792]{1,0:T(8,128)(2,1)S(1)}, bf16[128,1792]{1,0:T(8,128)(2,1)S(1)}, bf16[128,1792]{1,0:T(8,128)(2,1)S(1)}) custom-call(s32[4]{0:T(128)S(1)} %pad_add_fusion.places, bf16[512,448]{1,0:T(8,128)(2,1)S(1)} %bitcast.88, bf16[448,1792]{1,0:T(8,128)(2,1)S(1)} %pad_maximum_fusion.hidden_weight, ...), custom_call_target="tpu_custom_call" | custom-call | flops 1644167168 | bytes 6422528 | tf_op jit(solution)/shard_map/pallas_call | solution.py:211
  92.7 12.5 %fusion.2 = bf16[4,256,2048]{2,1,0:T(8,128)(2,1)} fusion(bf16[4,1792,256]{2,1,0:T(8,128)(2,1)} %bitcast.104, bf16[1792,2048]{1,0:T(8,128)(2,1)} %param.13), kind=kOutput, calls=%fused_computation.2 | convolution fusion | flops 7518289920 | bytes 15204352 | tf_op jit(solution)/shard_map/gkr,kn->grn/dot_general | solution.py:339
  109.3 5.1 %collective-permute-done.15 = bf16[128,1792]{1,0:T(8,128)(2,1)S(1)} collective-permute-done((bf16[128,1792]{1,0:T(8,128)(2,1)S(1)}, bf16[128,1792]{1,0:T(8,128)(2,1)S(1)}, u32[]{:S(2)}, u32[]{:S(2)}) %collective-permute-start.15) | collective-permute-done | bytes 458784 | tf_op jit(solution)/shard_map/ppermute | solution.py:97
  114.3 7.5 %collective-permute-done.14 = bf16[128,1792]{1,0:T(8,128)(2,1)S(1)} collective-permute-done((bf16[128,1792]{1,0:T(8,128)(2,1)S(1)}, bf16[128,1792]{1,0:T(8,128)(2,1)S(1)}, u32[]{:S(2)}, u32[]{:S(2)}) %collective-permute-start.14) | collective-permute-done | bytes 458784 | tf_op jit(solution)/shard_map/ppermute | solution.py:97
  124.9 2.9 %collective-permute-start.19 = (bf16[128,1792]{1,0:T(8,128)(2,1)S(1)}, bf16[128,1792]{1,0:T(8,128)(2,1)S(1)}, u32[]{:S(2)}, u32[]{:S(2)}) collective-permute-start(bf16[128,1792]{1,0:T(8,128)(2,1)S(1)} %add_convert_fusion.refs_0_), channel_id=1, source_target_pairs={{0,1},{1,0},{2,3},{3,2},{4,5},{5,4},{6,7},{7,6},{8,9},{9,8},{10,11... | collective-permute-start | bytes 1376264 | tf_op jit(solution)/shard_map/ppermute | solution.py:26
  127.8 3.3 %collective-permute-done.18.refs_3_ = bf16[128,1792]{1,0:T(8,128)(2,1)S(1)} collective-permute-done((bf16[128,1792]{1,0:T(8,128)(2,1)S(1)}, bf16[128,1792]{1,0:T(8,128)(2,1)S(1)}, u32[]{:S(2)}, u32[]{:S(2)}) %collective-permute-start.18) | collective-permute-done | bytes 458784 | tf_op jit(solution)/shard_map/ppermute | solution.py:97
  131.1 2.8 %collective-permute-start.22 = (bf16[128,1792]{1,0:T(8,128)(2,1)S(1)}, bf16[128,1792]{1,0:T(8,128)(2,1)S(1)}, u32[]{:S(2)}, u32[]{:S(2)}) collective-permute-start(bf16[128,1792]{1,0:T(8,128)(2,1)S(1)} %collective-permute-done.18.refs_3_), channel_id=1, source_target_pairs={{0,1},{1,0},{2,3},{3,2},{4,5},{5,4},{6,7},{7,6},{8,9},{9,8},{10,11... | collective-permute-start | bytes 1376264 | tf_op jit(solution)/shard_map/ppermute | solution.py:26
  133.9 2.3 %collective-permute-start.21 = (bf16[128,1792]{1,0:T(8,128)(2,1)S(1)}, bf16[128,1792]{1,0:T(8,128)(2,1)S(1)}, u32[]{:S(2)}, u32[]{:S(2)}) collective-permute-start(bf16[128,1792]{1,0:T(8,128)(2,1)S(1)} %collective-permute-done.17.refs_2_), channel_id=1, source_target_pairs={{0,1},{1,0},{2,3},{3,2},{4,5},{5,4},{6,7},{7,6},{8,9},{9,8},{10,11... | collective-permute-start | bytes 1376264 | tf_op jit(solution)/shard_map/ppermute | solution.py:26
  137.9 3.2 %collective-permute-start.20 = (bf16[128,1792]{1,0:T(8,128)(2,1)S(1)}, bf16[128,1792]{1,0:T(8,128)(2,1)}, u32[]{:S(2)}, u32[]{:S(2)}) collective-permute-start(bf16[128,1792]{1,0:T(8,128)(2,1)S(1)} %collective-permute-done.16.refs_1_), channel_id=1, source_target_pairs={{0,1},{1,0},{2,3},{3,2},{4,5},{5,4},{6,7},{7,6},{8,9},{9,8},{10,11... | collective-permute-start | bytes 1376264 | tf_op jit(solution)/shard_map/ppermute | solution.py:26
  142.6 3.0 %shard_map.124 = (bf16[2,256,1792]{2,1,0:T(8,128)(2,1)S(1)}, f32[2,256,1]{2,1,0:T(8,128)S(1)}) custom-call(s32[4]{0:T(128)S(1)} %pad_add_fusion.places, f32[1,1792]{1,0:T(1,128)S(1)} %reshape.130.gain, bf16[128,1792]{1,0:T(8,128)(2,1)S(1)} %add_convert_fusion.refs_0_, bf16[128,1792]{1,0:T(8,128)(2,1)S(1)} %collective-permute-done.16.refs_1_, ...), custom_call_target="tpu_custom_call" | custom-call | flops 3670016 | bytes 3670016 | tf_op jit(solution)/shard_map/pallas_call | solution.py:144
  145.6 5.4 %convolution_convert_fusion.1 = bf16[256,2048]{1,0:T(8,128)(2,1)S(1)} fusion(bf16[1792,2048]{1,0:T(8,128)(2,1)} %param.13, bf16[2,256,1792]{2,1,0:T(8,128)(2,1)S(1)} %get-tuple-element.61), kind=kOutput, calls=%fused_computation.4 | convolution fusion | flops 1879572480 | bytes 9306112 | tf_op jit(solution)/shard_map/dot_general | solution.py:22
  151.1 2.1 convolution_convert_fusion
  155.0 3.0 %collective-permute-start.24 = (bf16[128,2048]{1,0:T(8,128)(2,1)S(1)}, bf16[128,2048]{1,0:T(8,128)(2,1)}, u32[]{:S(2)}, u32[]{:S(2)}) collective-permute-start(bf16[128,2048]{1,0:T(8,128)(2,1)S(1)} %get-tuple-element.98), channel_id=1, source_target_pairs={{0,96},{32,0},{64,32},{96,64},{1,97},{33,1},{65,33},{97,65},{2,98}... | collective-permute-start | bytes 1572872 | tf_op jit(solution)/shard_map/ppermute | solution.py:364
  158.0 2.9 %shard_map.125 = (bf16[2,256,1792]{2,1,0:T(8,128)(2,1)S(1)}, f32[2,256,1]{2,1,0:T(8,128)S(1)}) custom-call(s32[4]{0:T(128)S(1)} %pad_add_fusion.places, f32[1,1792]{1,0:T(1,128)S(1)} %reshape.130.gain, bf16[128,1792]{1,0:T(8,128)(2,1)S(1)} %add_convert_fusion.refs_0_, bf16[128,1792]{1,0:T(8,128)(2,1)S(1)} %collective-permute-done.16.refs_1_, ...), custom_call_target="tpu_custom_call" | custom-call | flops 3670016 | bytes 3670016 | tf_op jit(solution)/shard_map/pallas_call | solution.py:144
  161.1 2.1 fusion.9
  163.2 2.1 fusion.12
  166.5 2.4 %collective-permute-done.25 = bf16[128,2048]{1,0:T(8,128)(2,1)S(1)} collective-permute-done((bf16[128,2048]{1,0:T(8,128)(2,1)S(1)}, bf16[128,2048]{1,0:T(8,128)(2,1)S(1)}, u32[]{:S(2)}, u32[]{:S(2)}) %collective-permute-start.25) | collective-permute-done | bytes 524320 | tf_op jit(solution)/shard_map/ppermute | solution.py:360
  171.7 6.2 %collective-permute-done.24 = bf16[128,2048]{1,0:T(8,128)(2,1)} collective-permute-done((bf16[128,2048]{1,0:T(8,128)(2,1)S(1)}, bf16[128,2048]{1,0:T(8,128)(2,1)}, u32[]{:S(2)}, u32[]{:S(2)}) %collective-permute-start.24) | collective-permute-done | bytes 524320 | tf_op jit(solution)/shard_map/ppermute | solution.py:364
  177.8 2.4 %collective-permute-done.23 = bf16[128,2048]{1,0:T(8,128)(2,1)} collective-permute-done((bf16[128,2048]{1,0:T(8,128)(2,1)S(1)}, bf16[128,2048]{1,0:T(8,128)(2,1)}, u32[]{:S(2)}, u32[]{:S(2)}) %collective-permute-start.23) | collective-permute-done | bytes 524320 | tf_op jit(solution)/shard_map/ppermute | solution.py:363
  184.4 4.7 %collective-permute-done.28 = f32[256]{0:T(256)S(1)} collective-permute-done((f32[256]{0:T(256)S(1)}, f32[256]{0:T(256)S(1)}, u32[]{:S(2)}, u32[]{:S(2)}) %collective-permute-start.28) | collective-permute-done | bytes 1056 | tf_op jit(solution)/shard_map/ppermute | solution.py:394
  189.1 2.4 %collective-permute-done.27 = f32[256]{0:T(256)S(1)} collective-permute-done((f32[256]{0:T(256)S(1)}, f32[256]{0:T(256)S(1)}, u32[]{:S(2)}, u32[]{:S(2)}) %collective-permute-start.27) | collective-permute-done | bytes 1056 | tf_op jit(solution)/shard_map/ppermute | solution.py:394
  194.8 12.1 %all_to_all.26 = f32[32,1,1024]{2,1,0:T(1,128)S(1)} all-to-all(f32[32,1,1024]{2,1,0:T(1,128)S(1)} %broadcast_in_dim.24), channel_id=1, replica_groups=mesh['group'=4,'x'=4,'z'=4,'core'=2] {'x','z','core'}, dimensions={0} | all-to-all | bytes 262144 | tf_op jit(solution)/shard_map/all_to_all | solution.py:72
  (136 shorter events, 49.0 us)
Async XLA Ops:
  10.6 16.8 %all-to-all-start = ((f32[32,1,288]{2,1,0:T(1,128)}), f32[32,1,288]{2,1,0:T(1,128)S(1)}, u32[]{:S(2)}, u32[]{:S(2)}) async-start(f32[32,1,288]{2,1,0:T(1,128)} %broadcast_in_dim.19), calls=%async_computation | async-start | bytes 98304 | tf_op jit(solution)/shard_map/all_to_all | solution.py:72
  20.1 72.6 %all-gather.2.cloned.1.call-start = ((), (), s32[]{:S(2)}) async-start(), calls=%async_computation.5 | async-start | bytes 3784704 | tf_op jit(solution)/shard_map/all_gather | solution.py:284
  20.1 12.3 %collective-permute-start = (bf16[224,256]{0,1:T(8,128)(2,1)S(1)}, bf16[224,256]{0,1:T(8,128)(2,1)S(1)}, u32[]{:S(2)}, u32[]{:S(2)}) collective-permute-start(bf16[224,256]{0,1:T(8,128)(2,1)S(1)} %get-tuple-element.42), channel_id=1, source_target_pairs={{0,0},{8,32},{16,64},{24,96},{32,8},{40,40},{48,72},{56,104},{64,1... | collective-permute-start | bytes 344072 | tf_op jit(solution)/shard_map/ppermute | solution.py:31
  33.8 13.2 %collective-permute-start.8 = (bf16[256,224]{1,0:T(8,128)(2,1)S(1)}, bf16[256,224]{1,0:T(8,128)(2,1)S(1)}, u32[]{:S(2)}, u32[]{:S(2)}) collective-permute-start(bf16[256,224]{1,0:T(8,128)(2,1)S(1)} %fusion.23), channel_id=1, source_target_pairs={{0,96},{32,0},{64,32},{96,64},{1,97},{33,1},{65,33},{97,65},{2,98}... | collective-permute-start | bytes 344072 | tf_op jit(solution)/shard_map/ppermute | solution.py:296
  37.2 9.7 %collective-permute-start.7 = (bf16[256,224]{1,0:T(8,128)(2,1)S(1)}, bf16[256,224]{1,0:T(8,128)(2,1)S(1)}, u32[]{:S(2)}, u32[]{:S(2)}) collective-permute-start(bf16[256,224]{1,0:T(8,128)(2,1)S(1)} %fusion.23), channel_id=1, source_target_pairs={{0,64},{32,96},{64,0},{96,32},{1,65},{33,97},{65,1},{97,33},{2,66}... | collective-permute-start | bytes 344072 | tf_op jit(solution)/shard_map/ppermute | solution.py:296
  37.2 9.7 %collective-permute-start.6 = (bf16[256,224]{1,0:T(8,128)(2,1)S(1)}, bf16[256,224]{1,0:T(8,128)(2,1)S(1)}, u32[]{:S(2)}, u32[]{:S(2)}) collective-permute-start(bf16[256,224]{1,0:T(8,128)(2,1)S(1)} %fusion.23), channel_id=1, source_target_pairs={{0,32},{32,64},{64,96},{96,0},{1,33},{33,65},{65,97},{97,1},{2,34}... | collective-permute-start | bytes 344072 | tf_op jit(solution)/shard_map/ppermute | solution.py:296
  38.8 18.5 %all-to-all-start.1 = ((bf16[32,4,1792]{2,1,0:T(4,128)(2,1)}), bf16[32,4,1792]{2,1,0:T(4,128)(2,1)S(1)}, u32[]{:S(2)}, u32[]{:S(2)}) async-start(bf16[32,4,1792]{2,1,0:T(4,128)(2,1)} %reshape.132), calls=%async_computation.1 | async-start | bytes 917504 | tf_op jit(solution)/shard_map/all_to_all | solution.py:313
  45.4 134.9 %reduce-scatter.2.cloned.1.call-start = ((), (), s32[]{:S(2)}) async-start(), calls=%async_computation.6 | async-start | bytes 5242880 | tf_op jit(solution)/shard_map/reduce_scatter | solution.py:343
  46.6 15.6 %collective-permute-start.4 = (bf16[224,1792]{1,0:T(8,128)(2,1)S(1)}, bf16[224,1792]{1,0:T(8,128)(2,1)S(1)}, u32[]{:S(2)}, u32[]{:S(2)}) collective-permute-start(bf16[224,1792]{1,0:T(8,128)(2,1)S(1)} %constant_dynamic-slice_fusion.5), channel_id=1, source_target_pairs={{0,1},{1,0},{2,3},{3,2},{4,5},{5,4},{6,7},{7,6},{8,9},{9,8},{10,11... | collective-permute-start | bytes 2408456 | tf_op jit(solution)/shard_map/ppermute | solution.py:26
  49.6 14.2 %collective-permute-start.5 = (bf16[224,1792]{1,0:T(8,128)(2,1)}, bf16[224,1792]{1,0:T(8,128)(2,1)}, u32[]{:S(2)}, u32[]{:S(2)}) collective-permute-start(bf16[224,1792]{1,0:T(8,128)(2,1)} %constant_dynamic-slice_fusion.4), channel_id=1, source_target_pairs={{0,1},{1,0},{2,3},{3,2},{4,5},{5,4},{6,7},{7,6},{8,9},{9,8},{10,11... | collective-permute-start | bytes 2408456 | tf_op jit(solution)/shard_map/ppermute | solution.py:26
  57.6 8.0 %collective-permute-start.3 = (bf16[32,1792]{1,0:T(8,128)(2,1)S(1)}, bf16[32,1792]{1,0:T(8,128)(2,1)S(1)}, u32[]{:S(2)}, u32[]{:S(2)}) collective-permute-start(bf16[32,1792]{1,0:T(8,128)(2,1)S(1)} %convolution_convert_fusion.3.refs_0_), channel_id=1, source_target_pairs={{0,96},{32,0},{64,32},{96,64},{1,97},{33,1},{65,33},{97,65},{2,98}... | collective-permute-start | bytes 344072 | tf_op jit(solution)/shard_map/ppermute | solution.py:324
  61.5 8.2 %collective-permute-start.1 = (bf16[32,1792]{1,0:T(8,128)(2,1)S(1)}, bf16[32,1792]{1,0:T(8,128)(2,1)S(1)}, u32[]{:S(2)}, u32[]{:S(2)}) collective-permute-start(bf16[32,1792]{1,0:T(8,128)(2,1)S(1)} %convolution_convert_fusion.3.refs_0_), channel_id=1, source_target_pairs={{0,32},{32,64},{64,96},{96,0},{1,33},{33,65},{65,97},{97,1},{2,34}... | collective-permute-start | bytes 344072 | tf_op jit(solution)/shard_map/ppermute | solution.py:324
  89.1 16.1 %collective-permute-start.10 = (bf16[128,1792]{1,0:T(8,128)(2,1)S(1)}, bf16[128,1792]{1,0:T(8,128)(2,1)S(1)}, u32[]{:S(2)}, u32[]{:S(2)}) collective-permute-start(bf16[128,1792]{1,0:T(8,128)(2,1)S(1)} %get-tuple-element.54), channel_id=1, source_target_pairs={{0,16},{1,5},{2,18},{3,7},{4,20},{5,1},{6,22},{7,3},{8,24},{9,13},... | collective-permute-start | bytes 1376264 | tf_op jit(solution)/shard_map/ppermute | solution.py:97
  90.0 15.2 %collective-permute-start.11 = (bf16[128,1792]{1,0:T(8,128)(2,1)S(1)}, bf16[128,1792]{1,0:T(8,128)(2,1)S(1)}, u32[]{:S(2)}, u32[]{:S(2)}) collective-permute-start(bf16[128,1792]{1,0:T(8,128)(2,1)S(1)} %get-tuple-element.55), channel_id=1, source_target_pairs={{0,8},{1,3},{2,10},{3,5},{4,12},{5,7},{6,14},{7,1},{8,16},{9,11},{... | collective-permute-start | bytes 1376264 | tf_op jit(solution)/shard_map/ppermute | solution.py:97
  91.1 14.2 %collective-permute-start.12 = (bf16[128,1792]{1,0:T(8,128)(2,1)S(1)}, bf16[128,1792]{1,0:T(8,128)(2,1)}, u32[]{:S(2)}, u32[]{:S(2)}) collective-permute-start(bf16[128,1792]{1,0:T(8,128)(2,1)S(1)} %get-tuple-element.56), channel_id=1, source_target_pairs={{0,24},{1,7},{2,26},{3,1},{4,28},{5,3},{6,30},{7,5},{8,0},{9,15},{... | collective-permute-start | bytes 1376264 | tf_op jit(solution)/shard_map/ppermute | solution.py:97
  106.5 7.8 %collective-permute-start.15 = (bf16[128,1792]{1,0:T(8,128)(2,1)S(1)}, bf16[128,1792]{1,0:T(8,128)(2,1)S(1)}, u32[]{:S(2)}, u32[]{:S(2)}) collective-permute-start(bf16[128,1792]{1,0:T(8,128)(2,1)S(1)} %fusion.25), channel_id=1, source_target_pairs={{0,6},{1,25},{2,0},{3,27},{4,2},{5,29},{6,4},{7,31},{8,14},{9,1},{... | collective-permute-start | bytes 1376264 | tf_op jit(solution)/shard_map/ppermute | solution.py:97
  108.0 13.9 %collective-permute-start.14 = (bf16[128,1792]{1,0:T(8,128)(2,1)S(1)}, bf16[128,1792]{1,0:T(8,128)(2,1)S(1)}, u32[]{:S(2)}, u32[]{:S(2)}) collective-permute-start(bf16[128,1792]{1,0:T(8,128)(2,1)S(1)} %fusion.25), channel_id=1, source_target_pairs={{0,2},{1,9},{2,4},{3,11},{4,6},{5,13},{6,0},{7,15},{8,10},{9,17},{... | collective-permute-start | bytes 1376264 | tf_op jit(solution)/shard_map/ppermute | solution.py:97
  108.1 13.8 %collective-permute-start.13 = (bf16[128,1792]{1,0:T(8,128)(2,1)S(1)}, bf16[128,1792]{1,0:T(8,128)(2,1)S(1)}, u32[]{:S(2)}, u32[]{:S(2)}) collective-permute-start(bf16[128,1792]{1,0:T(8,128)(2,1)S(1)} %fusion.25), channel_id=1, source_target_pairs={{0,4},{1,17},{2,6},{3,19},{4,0},{5,21},{6,2},{7,23},{8,12},{9,25},... | collective-permute-start | bytes 1376264 | tf_op jit(solution)/shard_map/ppermute | solution.py:97
  123.7 10.2 %collective-permute-start.17 = (bf16[128,1792]{1,0:T(8,128)(2,1)S(1)}, bf16[128,1792]{1,0:T(8,128)(2,1)S(1)}, u32[]{:S(2)}, u32[]{:S(2)}) collective-permute-start(bf16[128,1792]{1,0:T(8,128)(2,1)S(1)} %add_convert_fusion.refs_0_), channel_id=1, source_target_pairs={{0,16},{1,5},{2,18},{3,7},{4,20},{5,1},{6,22},{7,3},{8,24},{9,13},... | collective-permute-start | bytes 1376264 | tf_op jit(solution)/shard_map/ppermute | solution.py:97
  124.5 13.4 %collective-permute-start.16 = (bf16[128,1792]{1,0:T(8,128)(2,1)S(1)}, bf16[128,1792]{1,0:T(8,128)(2,1)S(1)}, u32[]{:S(2)}, u32[]{:S(2)}) collective-permute-start(bf16[128,1792]{1,0:T(8,128)(2,1)S(1)} %add_convert_fusion.refs_0_), channel_id=1, source_target_pairs={{0,8},{1,3},{2,10},{3,5},{4,12},{5,7},{6,14},{7,1},{8,16},{9,11},{... | collective-permute-start | bytes 1376264 | tf_op jit(solution)/shard_map/ppermute | solution.py:97
  124.9 17.0 %collective-permute-start.19 = (bf16[128,1792]{1,0:T(8,128)(2,1)S(1)}, bf16[128,1792]{1,0:T(8,128)(2,1)S(1)}, u32[]{:S(2)}, u32[]{:S(2)}) collective-permute-start(bf16[128,1792]{1,0:T(8,128)(2,1)S(1)} %add_convert_fusion.refs_0_), channel_id=1, source_target_pairs={{0,1},{1,0},{2,3},{3,2},{4,5},{5,4},{6,7},{7,6},{8,9},{9,8},{10,11... | collective-permute-start | bytes 1376264 | tf_op jit(solution)/shard_map/ppermute | solution.py:26
  131.1 10.7 %collective-permute-start.22 = (bf16[128,1792]{1,0:T(8,128)(2,1)S(1)}, bf16[128,1792]{1,0:T(8,128)(2,1)S(1)}, u32[]{:S(2)}, u32[]{:S(2)}) collective-permute-start(bf16[128,1792]{1,0:T(8,128)(2,1)S(1)} %collective-permute-done.18.refs_3_), channel_id=1, source_target_pairs={{0,1},{1,0},{2,3},{3,2},{4,5},{5,4},{6,7},{7,6},{8,9},{9,8},{10,11... | collective-permute-start | bytes 1376264 | tf_op jit(solution)/shard_map/ppermute | solution.py:26
  133.9 7.9 %collective-permute-start.21 = (bf16[128,1792]{1,0:T(8,128)(2,1)S(1)}, bf16[128,1792]{1,0:T(8,128)(2,1)S(1)}, u32[]{:S(2)}, u32[]{:S(2)}) collective-permute-start(bf16[128,1792]{1,0:T(8,128)(2,1)S(1)} %collective-permute-done.17.refs_2_), channel_id=1, source_target_pairs={{0,1},{1,0},{2,3},{3,2},{4,5},{5,4},{6,7},{7,6},{8,9},{9,8},{10,11... | collective-permute-start | bytes 1376264 | tf_op jit(solution)/shard_map/ppermute | solution.py:26
  153.3 13.2 %collective-permute-start.26 = (bf16[128,2048]{1,0:T(8,128)(2,1)S(1)}, bf16[128,2048]{1,0:T(8,128)(2,1)S(1)}, u32[]{:S(2)}, u32[]{:S(2)}) collective-permute-start(bf16[128,2048]{1,0:T(8,128)(2,1)S(1)} %get-tuple-element.96), channel_id=1, source_target_pairs={{0,96},{32,0},{64,32},{96,64},{1,97},{33,1},{65,33},{97,65},{2,98}... | collective-permute-start | bytes 1572872 | tf_op jit(solution)/shard_map/ppermute | solution.py:361
  154.9 14.0 %collective-permute-start.25 = (bf16[128,2048]{1,0:T(8,128)(2,1)S(1)}, bf16[128,2048]{1,0:T(8,128)(2,1)S(1)}, u32[]{:S(2)}, u32[]{:S(2)}) collective-permute-start(bf16[128,2048]{1,0:T(8,128)(2,1)S(1)} %get-tuple-element.97), channel_id=1, source_target_pairs={{0,32},{32,64},{64,96},{96,0},{1,33},{33,65},{65,97},{97,1},{2,34}... | collective-permute-start | bytes 1572872 | tf_op jit(solution)/shard_map/ppermute | solution.py:360
  155.0 22.8 %collective-permute-start.24 = (bf16[128,2048]{1,0:T(8,128)(2,1)S(1)}, bf16[128,2048]{1,0:T(8,128)(2,1)}, u32[]{:S(2)}, u32[]{:S(2)}) collective-permute-start(bf16[128,2048]{1,0:T(8,128)(2,1)S(1)} %get-tuple-element.98), channel_id=1, source_target_pairs={{0,96},{32,0},{64,32},{96,64},{1,97},{33,1},{65,33},{97,65},{2,98}... | collective-permute-start | bytes 1572872 | tf_op jit(solution)/shard_map/ppermute | solution.py:364
  158.0 22.2 %collective-permute-start.23 = (bf16[128,2048]{1,0:T(8,128)(2,1)S(1)}, bf16[128,2048]{1,0:T(8,128)(2,1)}, u32[]{:S(2)}, u32[]{:S(2)}) collective-permute-start(bf16[128,2048]{1,0:T(8,128)(2,1)S(1)} %get-tuple-element.99), channel_id=1, source_target_pairs={{0,32},{32,64},{64,96},{96,0},{1,33},{33,65},{65,97},{97,1},{2,34}... | collective-permute-start | bytes 1572872 | tf_op jit(solution)/shard_map/ppermute | solution.py:363
  170.2 21.3 %collective-permute-start.31 = (bf16[128,2048]{1,0:T(8,128)(2,1)}, bf16[128,2048]{1,0:T(8,128)(2,1)}, u32[]{:S(2)}, u32[]{:S(2)}) collective-permute-start(bf16[128,2048]{1,0:T(8,128)(2,1)} %get-tuple-element.90), channel_id=1, source_target_pairs={{0,96},{32,0},{64,32},{96,64},{1,97},{33,1},{65,33},{97,65},{2,98}... | collective-permute-start | bytes 1572872 | tf_op jit(solution)/shard_map/ppermute | solution.py:371
  170.5 21.0 %collective-permute-start.30 = (bf16[128,2048]{1,0:T(8,128)(2,1)}, bf16[128,2048]{1,0:T(8,128)(2,1)}, u32[]{:S(2)}, u32[]{:S(2)}) collective-permute-start(bf16[128,2048]{1,0:T(8,128)(2,1)} %get-tuple-element.91), channel_id=1, source_target_pairs={{0,32},{32,64},{64,96},{96,0},{1,33},{33,65},{65,97},{97,1},{2,34}... | collective-permute-start | bytes 1572872 | tf_op jit(solution)/shard_map/ppermute | solution.py:370
  180.3 8.8 %collective-permute-start.28 = (f32[256]{0:T(256)S(1)}, f32[256]{0:T(256)S(1)}, u32[]{:S(2)}, u32[]{:S(2)}) collective-permute-start(f32[256]{0:T(256)S(1)} %pad_maximum_fusion.8), channel_id=1, source_target_pairs={{0,96},{32,0},{64,32},{96,64},{1,97},{33,1},{65,33},{97,65},{2,98}... | collective-permute-start | bytes 3080 | tf_op jit(solution)/shard_map/ppermute | solution.py:394
  180.7 10.8 %collective-permute-start.27 = (f32[256]{0:T(256)S(1)}, f32[256]{0:T(256)S(1)}, u32[]{:S(2)}, u32[]{:S(2)}) collective-permute-start(f32[256]{0:T(256)S(1)} %pad_maximum_fusion.7), channel_id=1, source_target_pairs={{0,32},{32,64},{64,96},{96,0},{1,33},{33,65},{65,97},{97,1},{2,34}... | collective-permute-start | bytes 3080 | tf_op jit(solution)/shard_map/ppermute | solution.py:394
  181.8 9.7 %collective-permute-start.29 = (f32[256]{0:T(256)S(1)}, f32[256]{0:T(256)S(1)}, u32[]{:S(2)}, u32[]{:S(2)}) collective-permute-start(f32[256]{0:T(256)S(1)} %get-tuple-element.83), channel_id=1, source_target_pairs={{0,64},{32,96},{64,0},{96,32},{1,65},{33,97},{65,1},{97,33},{2,66}... | collective-permute-start | bytes 3080 | tf_op jit(solution)/shard_map/ppermute | solution.py:394
  (8 other events, 41.3 us)
Sparse Core Ops, SparseCore 0:
  33.4 50.0 all-gather.1
  105.4 44.3 reduce-scatter.1
